TPU v7x, 512 devices: a whole 4x4x16 slice. The times are simulated.
512 devices in a mesh: dp: 16 (over z), seq: 32 (over x, y, core).
Axes of the slice: x: 4, y: 4, z: 16, core: 2. Of those that a mesh axis runs over, the one named last changes fastest.
Arguments:
- inputs: bfloat16 [16, 32, 256, 256], P('dp', 'seq'), may hold values from -6 to 6
- cotangent: bfloat16 [16, 32, 256, 256], P('dp', 'seq'), may hold values from -6 to 6
- lengths: int32 [16, 8], P('dp'), may hold values from 1 to 2048, 8192 in all within a row
- placed: int32 [16, 32], P('dp'), may hold values from 0 to 31, each once within a row
- conv_weight: float32 [51, 256], replicated, may hold values from -0.875 to 0.875
- norm_gain: float32 [256], replicated, may hold values from 0.5 to 1.5
- up_weight: bfloat16 [256, 1024], replicated, may hold values from -0.375 to 0.375
- down_weight: bfloat16 [1024, 256], replicated, may hold values from -0.1875 to 0.1875
Outputs:
- outputs: bfloat16 [16, 32, 256, 256], P('dp', 'seq')
- grad_inputs: bfloat16 [16, 32, 256, 256], P('dp', 'seq')
- grad_kernel: bfloat16 [51, 256], replicated
- grad_gain: bfloat16 [256], replicated
- grad_up: bfloat16 [256, 1024], replicated
- grad_down: bfloat16 [1024, 256], replicated
Inputs may be any that keep to these rules, and one draw needn't show every extreme that they name: `lengths`: each trace has at least one step and together they fill the group's 256 * 32 steps. `placed`: each row is a permutation of the span numbers.
All inputs are finite; a program needn't handle non-finite values.
Results may differ from a plain program's by a relative error of at most 0.0061.
Values may be sent and summed in bfloat16 or wider, within the bound.
A program may use at most 64 MiB of HBM per device.

v0:
```python
import math

import jax
import jax.numpy as jnp
from jax import lax
from jax.sharding import PartitionSpec as P

epsilon = 1e-05


def depth_rows(positions, lengths):
    trace_ends = jnp.cumsum(lengths)
    trace_start = jnp.sum(
        jnp.where(trace_ends[None, :] <= positions[:, None], lengths[None, :], 0), axis=1
    )
    return positions - trace_start


def contract_rows(left, right):
    return lax.dot_general(
        left, right, (((0,), (0,)), ((), ())), preferred_element_type=jnp.float32
    )


def contract_cols(left, right):
    return lax.dot_general(
        left, right, (((1,), (1,)), ((), ())), preferred_element_type=jnp.float32
    )


def per_device(inputs, cotangent, lengths, placed, conv_weight, norm_gain, up_weight, down_weight):
    row_count = inputs.shape[2]
    channels = inputs.shape[3]
    kernel = conv_weight.shape[0]
    reach_rows = kernel - 1
    spans = lax.axis_size("seq")
    groups = lax.axis_size("dp")
    current = inputs.reshape(row_count, channels)
    upstream = cotangent.reshape(row_count, channels)
    my_slot = lax.axis_index("seq")
    order_row = placed[0]
    slot_ids = jnp.arange(spans, dtype=jnp.int32)
    my_span = jnp.sum(jnp.where(slot_ids == my_slot, order_row, 0))
    before_slot = jnp.sum(jnp.where(order_row == my_span - 1, slot_ids, 0))
    after_slot = jnp.sum(jnp.where(order_row == my_span + 1, slot_ids, 0))
    has_after = my_span < spans - 1
    positions = my_span * row_count + jnp.arange(row_count + reach_rows, dtype=jnp.int32)
    depth_ext = depth_rows(positions, lengths[0])
    depth = depth_ext[:row_count]
    tail_rows = current[row_count - reach_rows :]
    arrived = lax.all_gather(tail_rows[None], "seq", axis=0, tiled=True)
    halo_x = lax.dynamic_index_in_dim(arrived, before_slot, 0, keepdims=False)
    extended = jnp.concatenate([halo_x, current], axis=0)
    conv_out = jnp.zeros((row_count, channels), jnp.float32)
    for offset in range(kernel):
        window = extended[reach_rows - offset : reach_rows - offset + row_count].astype(jnp.float32)
        conv_out = conv_out + jnp.where(
            (offset <= depth)[:, None], conv_weight[offset] * window, 0.0
        )
    centre = jnp.mean(conv_out, axis=-1, keepdims=True)
    centered = conv_out - centre
    variance = jnp.mean(centered * centered, axis=-1, keepdims=True)
    inv_std = lax.rsqrt(variance + epsilon)
    normed = centered * inv_std
    scaled = (normed * norm_gain).astype(jnp.bfloat16)
    hidden = jnp.dot(scaled, up_weight, preferred_element_type=jnp.float32)
    activated = jax.nn.gelu(hidden).astype(jnp.bfloat16)
    result = (
        current.astype(jnp.float32)
        + jnp.dot(activated, down_weight, preferred_element_type=jnp.float32)
    ).astype(jnp.bfloat16)
    grad_down = contract_rows(activated, upstream)
    grad_act = contract_cols(upstream, down_weight)
    pullback = jax.vjp(jax.nn.gelu, hidden)[1]
    grad_hidden = pullback(grad_act)[0].astype(jnp.bfloat16)
    grad_up = contract_rows(scaled, grad_hidden)
    grad_normed = contract_cols(grad_hidden, up_weight)
    grad_gain = jnp.sum(grad_normed * normed, axis=0)
    weighted = grad_normed * norm_gain
    grad_conv_out = inv_std * (
        weighted
        - jnp.mean(weighted, axis=-1, keepdims=True)
        - normed * jnp.mean(weighted * normed, axis=-1, keepdims=True)
    )
    head_rows = grad_conv_out[:reach_rows]
    arrived_back = lax.all_gather(
        head_rows[None].astype(jnp.bfloat16), "seq", axis=0, tiled=True
    ).astype(jnp.float32)
    halo_grad = jnp.where(
        has_after, lax.dynamic_index_in_dim(arrived_back, after_slot, 0, keepdims=False), 0.0
    )
    grad_extended = jnp.concatenate([grad_conv_out, halo_grad], axis=0)
    grad_through = jnp.zeros((row_count, channels), jnp.float32)
    kernel_rows = []
    for offset in range(kernel):
        ahead = grad_extended[offset : offset + row_count]
        grad_through = grad_through + jnp.where(
            (offset <= depth_ext[offset : offset + row_count])[:, None],
            conv_weight[offset] * ahead,
            0.0,
        )
        window = extended[reach_rows - offset : reach_rows - offset + row_count].astype(jnp.float32)
        kernel_rows.append(
            jnp.sum(jnp.where((offset <= depth)[:, None], grad_conv_out * window, 0.0), axis=0)
        )
    grad_kernel = jnp.stack(kernel_rows, axis=0)
    grad_series = (upstream.astype(jnp.float32) + grad_through).astype(jnp.bfloat16)
    summed_up, summed_down, summed_kernel, summed_gain = lax.psum(
        (grad_up, grad_down, grad_kernel, grad_gain), ("dp", "seq")
    )
    factor = 1.0 / math.sqrt(groups * spans * row_count)
    return (
        result.reshape(inputs.shape),
        grad_series.reshape(inputs.shape),
        (summed_kernel * factor).astype(jnp.bfloat16),
        (summed_gain * factor).astype(jnp.bfloat16),
        (summed_up * factor).astype(jnp.bfloat16),
        (summed_down * factor).astype(jnp.bfloat16),
    )


def solution(mesh):
    placed = (
        P("dp", "seq", None, None),
        P("dp", "seq", None, None),
        P("dp", None),
        P("dp", None),
        P(),
        P(),
        P(),
        P(),
    )
    return jax.shard_map(
        per_device,
        mesh=mesh,
        in_specs=placed,
        out_specs=(P("dp", "seq", None, None), P("dp", "seq", None, None), P(), P(), P(), P()),
        check_vma=False,
    )
```

profile of v0, /device:TPU:1, one launch (start us, length us, event | category | flops | bytes accessed | tf_op | source)
XLA Modules:
  0.0 549.1 jit_solution(6628510177465594853)
XLA Ops:
  7.2 0.0 all-reduce.4.cloned.1.call-start
  7.2 0.9 fusion.489
  8.3 1.0 fusion.487
  9.3 1.3 fusion.472
  11.3 0.8 reduce-window.8
  12.1 0.7 select_reduce_fusion
  12.9 0.7 slice_compare_fusion.47
  13.6 0.7 slice_compare_fusion.48
  14.3 1.0 fusion.488
  15.5 0.7 slice_compare_fusion.49
  16.1 0.7 slice_compare_fusion.44
  16.8 28.7 %all-gather = bf16[32,1,50,256]{3,2,1,0:T(8,128)(2,1)S(1)} all-gather(bf16[1,1,50,256]{3,2,1,0:T(8,128)(2,1)S(1)} %slice.719), channel_id=2, replica_groups=mesh['dp'=16,'seq'=32] {'seq'}, dimensions={0}, use_global_device_ids=true | all-gather | bytes 844800 | tf_op jit(solution)/shard_map/all_gather | solution.py:51
  46.8 0.6 fusion.474
  49.8 6.9 %fusion.477 = (f32[256]{0:T(256)S(1)}, f32[256,256]{1,0:T(8,128)S(1)}, bf16[256,256]{1,0:T(8,128)(2,1)S(1)}, bf16[256,256]{1,0:T(8,128)(2,1)S(1)}, bf16[256,256]...) fusion(bf16[256,256]{1,0:T(8,128)(2,1)S(1)} %bitcast.138, ...), kind=kLoop, calls=%fused_computation.854 | loop fusion | flops 23723776 | bytes 1533696 | tf_op jit(solution)/shard_map/reduce_sum | solution.py:60
  56.7 0.2 multiply_reduce_fusion.2
  56.9 0.7 copy-done.55
  57.6 0.4 fusion.476
  58.0 0.5 copy-done.5
  58.5 1.6 fusion.462
  60.1 0.9 fusion.8
  60.9 1.4 fusion.475
  62.4 0.0 all-reduce.4.cloned.1.call-update
  62.4 0.9 multiply_reduce_fusion
  64.5 0.7 slice_compare_fusion.46
  65.2 0.7 slice_compare_fusion.45
  66.0 0.7 copy-done.56
  66.6 2.1 fusion.208
  68.8 1.6 fusion.71
  70.4 1.6 fusion.92
  72.0 1.6 fusion.134
  73.6 1.6 fusion.152
  75.3 0.9 fusion.170
  76.3 0.9 fusion.188
  77.2 25.3 %all-gather.2 = bf16[32,50,256]{2,1,0:T(8,128)(2,1)S(1)} all-gather(bf16[1,50,256]{2,1,0:T(8,128)(2,1)S(1)} %fusion.470), channel_id=3, replica_groups=mesh['dp'=16,'seq'=32] {'seq'}, dimensions={0}, use_global_device_ids=true | all-gather | bytes 844800 | tf_op jit(solution)/shard_map/all_gather | solution.py:86
  103.3 0.6 copy-done.58
  103.8 0.1 copy-done.86
  103.9 2.2 fusion.86
  106.5 0.3 copy-done.88
  107.1 2.2 stack.207
  109.4 106.4 %all-reduce = (f32[51,256]{1,0:T(8,128)S(1)}, f32[256]{0:T(256)S(1)}) all-reduce(f32[51,256]{1,0:T(8,128)S(1)} %stack.207, f32[256]{0:T(256)} %get-tuple-element.6), channel_id=1, replica_groups=mesh['dp'=16,'seq'=32] {'dp','seq'}, use_global_device_ids=true, to_apply=%region_60.61 | all-reduce | flops 13312 | bytes 106496 | tf_op jit(solution)/shard_map/psum | solution.py:108
  215.8 0.6 multiply_convert_fusion.4
  216.4 0.5 multiply_convert_fusion.5
  217.9 2.2 fusion.1
  220.4 0.3 copy-done.8
  220.7 7.3 %fusion.468 = bf16[1,1,256,256]{3,2,1,0:T(8,128)(2,1)} fusion(f32[50,256]{1,0:T(8,128)S(1)} %fusion.469, f32[256,256]{1,0:T(8,128)S(1)} %get-tuple-element.66, f32[256]{0:T(256)S(1)} %bitcast.245, pred[256]{0:T(512)(128)(4,1)} %get-tuple-element.181, f32[256]{0:T(256)S(1)} %bitcast.247, pred[256]{0:T(512)(128)(4,1)} %get-tuple-element.182, ...), kind=kLoop, calls=%fused_computation.730 | loop fusion | flops 13434880 | bytes 640768 | tf_op jit(solution)/shard_map/reshape | solution.py:114
  228.0 311.1 %all-reduce.4.cloned.1.call-done = (f32[256,1024]{1,0:T(8,128)}, f32[1024,256]{1,0:T(8,128)}) async-done(((f32[256,1024]{1,0:T(8,128)}, f32[1024,256]{1,0:T(8,128)}), (f32[256,1024]{1,0:T(8,128)}, f32[1024,256]{1,0:T(8,128)})) %all-reduce.4.cloned.1.call-update) | async-done | bytes 2097168 | tf_op jit(solution)/shard_map/psum | solution.py:108
  539.1 2.2 multiply_convert_fusion.1
  541.3 0.9 multiply_convert_fusion
  (290 shorter events, 0.7 us)
Async XLA Ops:
  7.2 49.8 %copy-start = (bf16[256,1024]{1,0:T(8,128)(2,1)S(1)}, bf16[256,1024]{1,0:T(8,128)(2,1)}, u32[]{:S(2)}) copy-start(bf16[256,1024]{1,0:T(8,128)(2,1)} %param.14) | copy-start | bytes 1572868
  7.2 9.6 %copy-start.1 = (bf16[1,1,256,256]{3,2,1,0:T(8,128)(2,1)S(1)}, bf16[1,1,256,256]{3,2,1,0:T(8,128)(2,1)}, u32[]{:S(2)}) copy-start(bf16[1,1,256,256]{3,2,1,0:T(8,128)(2,1)} %param.8) | copy-start | bytes 393220
  7.2 531.9 %all-reduce.4.cloned.1.call-start = ((), (), s32[]{:S(2)}) async-start(), calls=%async_computation | async-start | bytes 4194304 | tf_op jit(solution)/shard_map/psum | solution.py:108
  8.2 41.3 %copy-start.29 = (f32[1,256]{1,0:T(1,128)}, f32[1,256]{1,0:T(1,128)S(1)}, u32[]{:S(2)}) copy-start(f32[1,256]{1,0:T(1,128)S(1)} %get-tuple-element.115) | copy-start | bytes 3076
  8.2 41.3 %copy-start.31 = (f32[1,256]{1,0:T(1,128)}, f32[1,256]{1,0:T(1,128)S(1)}, u32[]{:S(2)}) copy-start(f32[1,256]{1,0:T(1,128)S(1)} %get-tuple-element.116) | copy-start | bytes 3076
  8.2 41.3 %copy-start.33 = (f32[1,256]{1,0:T(1,128)}, f32[1,256]{1,0:T(1,128)S(1)}, u32[]{:S(2)}) copy-start(f32[1,256]{1,0:T(1,128)S(1)} %get-tuple-element.117) | copy-start | bytes 3076
  8.2 41.3 %copy-start.35 = (f32[1,256]{1,0:T(1,128)}, f32[1,256]{1,0:T(1,128)S(1)}, u32[]{:S(2)}) copy-start(f32[1,256]{1,0:T(1,128)S(1)} %get-tuple-element.118) | copy-start | bytes 3076
  8.2 41.3 %copy-start.37 = (f32[1,256]{1,0:T(1,128)}, f32[1,256]{1,0:T(1,128)S(1)}, u32[]{:S(2)}) copy-start(f32[1,256]{1,0:T(1,128)S(1)} %get-tuple-element.119) | copy-start | bytes 3076
  8.2 41.3 %copy-start.39 = (f32[1,256]{1,0:T(1,128)}, f32[1,256]{1,0:T(1,128)S(1)}, u32[]{:S(2)}) copy-start(f32[1,256]{1,0:T(1,128)S(1)} %get-tuple-element.120) | copy-start | bytes 3076
  8.2 41.3 %copy-start.41 = (f32[1,256]{1,0:T(1,128)}, f32[1,256]{1,0:T(1,128)S(1)}, u32[]{:S(2)}) copy-start(f32[1,256]{1,0:T(1,128)S(1)} %get-tuple-element.121) | copy-start | bytes 3076
  8.3 41.3 %copy-start.43 = (f32[1,256]{1,0:T(1,128)}, f32[1,256]{1,0:T(1,128)S(1)}, u32[]{:S(2)}) copy-start(f32[1,256]{1,0:T(1,128)S(1)} %get-tuple-element.122) | copy-start | bytes 3076
  8.3 41.3 %copy-start.45 = (f32[1,256]{1,0:T(1,128)}, f32[1,256]{1,0:T(1,128)S(1)}, u32[]{:S(2)}) copy-start(f32[1,256]{1,0:T(1,128)S(1)} %get-tuple-element.123) | copy-start | bytes 3076
  8.3 41.3 %copy-start.47 = (f32[1,256]{1,0:T(1,128)}, f32[1,256]{1,0:T(1,128)S(1)}, u32[]{:S(2)}) copy-start(f32[1,256]{1,0:T(1,128)S(1)} %get-tuple-element.124) | copy-start | bytes 3076
  8.3 41.3 %copy-start.49 = (f32[1,256]{1,0:T(1,128)}, f32[1,256]{1,0:T(1,128)S(1)}, u32[]{:S(2)}) copy-start(f32[1,256]{1,0:T(1,128)S(1)} %get-tuple-element.125) | copy-start | bytes 3076
  8.3 41.3 %copy-start.51 = (f32[1,256]{1,0:T(1,128)}, f32[1,256]{1,0:T(1,128)S(1)}, u32[]{:S(2)}) copy-start(f32[1,256]{1,0:T(1,128)S(1)} %get-tuple-element.126) | copy-start | bytes 3076
  8.3 41.3 %copy-start.53 = (f32[1,256]{1,0:T(1,128)}, f32[1,256]{1,0:T(1,128)S(1)}, u32[]{:S(2)}) copy-start(f32[1,256]{1,0:T(1,128)S(1)} %get-tuple-element.127) | copy-start | bytes 3076
  13.6 36.0 %copy-start.59 = (pred[256]{0:T(512)(128)(4,1)}, pred[256]{0:T(512)(128)(4,1)S(1)}, u32[]{:S(2)}) copy-start(pred[256]{0:T(512)(128)(4,1)S(1)} %get-tuple-element.169) | copy-start | bytes 772
  13.6 36.0 %copy-start.61 = (pred[256]{0:T(512)(128)(4,1)}, pred[256]{0:T(512)(128)(4,1)S(1)}, u32[]{:S(2)}) copy-start(pred[256]{0:T(512)(128)(4,1)S(1)} %get-tuple-element.170) | copy-start | bytes 772
  13.6 36.0 %copy-start.63 = (pred[256]{0:T(512)(128)(4,1)}, pred[256]{0:T(512)(128)(4,1)S(1)}, u32[]{:S(2)}) copy-start(pred[256]{0:T(512)(128)(4,1)S(1)} %get-tuple-element.171) | copy-start | bytes 772
  13.6 36.0 %copy-start.65 = (pred[256]{0:T(512)(128)(4,1)}, pred[256]{0:T(512)(128)(4,1)S(1)}, u32[]{:S(2)}) copy-start(pred[256]{0:T(512)(128)(4,1)S(1)} %get-tuple-element.172) | copy-start | bytes 772
  13.6 36.0 %copy-start.67 = (pred[256]{0:T(512)(128)(4,1)}, pred[256]{0:T(512)(128)(4,1)S(1)}, u32[]{:S(2)}) copy-start(pred[256]{0:T(512)(128)(4,1)S(1)} %get-tuple-element.173) | copy-start | bytes 772
  13.6 36.0 %copy-start.69 = (pred[256]{0:T(512)(128)(4,1)}, pred[256]{0:T(512)(128)(4,1)S(1)}, u32[]{:S(2)}) copy-start(pred[256]{0:T(512)(128)(4,1)S(1)} %get-tuple-element.174) | copy-start | bytes 772
  13.6 36.0 %copy-start.71 = (pred[256]{0:T(512)(128)(4,1)}, pred[256]{0:T(512)(128)(4,1)S(1)}, u32[]{:S(2)}) copy-start(pred[256]{0:T(512)(128)(4,1)S(1)} %get-tuple-element.167) | copy-start | bytes 772
  13.6 36.0 %copy-start.73 = (pred[256]{0:T(512)(128)(4,1)}, pred[256]{0:T(512)(128)(4,1)S(1)}, u32[]{:S(2)}) copy-start(pred[256]{0:T(512)(128)(4,1)S(1)} %get-tuple-element.168) | copy-start | bytes 772
  14.3 35.3 %copy-start.75 = (pred[256]{0:T(512)(128)(4,1)}, pred[256]{0:T(512)(128)(4,1)S(1)}, u32[]{:S(2)}) copy-start(pred[256]{0:T(512)(128)(4,1)S(1)} %get-tuple-element.162) | copy-start | bytes 772
  14.3 35.4 %copy-start.77 = (pred[256]{0:T(512)(128)(4,1)}, pred[256]{0:T(512)(128)(4,1)S(1)}, u32[]{:S(2)}) copy-start(pred[256]{0:T(512)(128)(4,1)S(1)} %get-tuple-element.163) | copy-start | bytes 772
  14.3 35.4 %copy-start.79 = (pred[256]{0:T(512)(128)(4,1)}, pred[256]{0:T(512)(128)(4,1)S(1)}, u32[]{:S(2)}) copy-start(pred[256]{0:T(512)(128)(4,1)S(1)} %get-tuple-element.164) | copy-start | bytes 772
  14.3 35.4 %copy-start.81 = (pred[256]{0:T(512)(128)(4,1)}, pred[256]{0:T(512)(128)(4,1)S(1)}, u32[]{:S(2)}) copy-start(pred[256]{0:T(512)(128)(4,1)S(1)} %get-tuple-element.165) | copy-start | bytes 772
  15.4 34.3 %copy-start.7 = (f32[1,256]{1,0:T(1,128)}, f32[1,256]{1,0:T(1,128)S(1)}, u32[]{:S(2)}) copy-start(f32[1,256]{1,0:T(1,128)S(1)} %get-tuple-element.104) | copy-start | bytes 3076
  15.4 34.3 %copy-start.9 = (f32[1,256]{1,0:T(1,128)}, f32[1,256]{1,0:T(1,128)S(1)}, u32[]{:S(2)}) copy-start(f32[1,256]{1,0:T(1,128)S(1)} %get-tuple-element.105) | copy-start | bytes 3076
  15.4 34.3 %copy-start.11 = (f32[1,256]{1,0:T(1,128)}, f32[1,256]{1,0:T(1,128)S(1)}, u32[]{:S(2)}) copy-start(f32[1,256]{1,0:T(1,128)S(1)} %get-tuple-element.106) | copy-start | bytes 3076
  15.4 34.3 %copy-start.13 = (f32[1,256]{1,0:T(1,128)}, f32[1,256]{1,0:T(1,128)S(1)}, u32[]{:S(2)}) copy-start(f32[1,256]{1,0:T(1,128)S(1)} %get-tuple-element.107) | copy-start | bytes 3076
  15.4 34.3 %copy-start.15 = (f32[1,256]{1,0:T(1,128)}, f32[1,256]{1,0:T(1,128)S(1)}, u32[]{:S(2)}) copy-start(f32[1,256]{1,0:T(1,128)S(1)} %get-tuple-element.108) | copy-start | bytes 3076
  15.4 34.3 %copy-start.17 = (f32[1,256]{1,0:T(1,128)}, f32[1,256]{1,0:T(1,128)S(1)}, u32[]{:S(2)}) copy-start(f32[1,256]{1,0:T(1,128)S(1)} %get-tuple-element.109) | copy-start | bytes 3076
  15.4 34.3 %copy-start.19 = (f32[1,256]{1,0:T(1,128)}, f32[1,256]{1,0:T(1,128)S(1)}, u32[]{:S(2)}) copy-start(f32[1,256]{1,0:T(1,128)S(1)} %get-tuple-element.110) | copy-start | bytes 3076
  15.4 34.3 %copy-start.21 = (f32[1,256]{1,0:T(1,128)}, f32[1,256]{1,0:T(1,128)S(1)}, u32[]{:S(2)}) copy-start(f32[1,256]{1,0:T(1,128)S(1)} %get-tuple-element.111) | copy-start | bytes 3076
  15.4 34.3 %copy-start.23 = (f32[1,256]{1,0:T(1,128)}, f32[1,256]{1,0:T(1,128)S(1)}, u32[]{:S(2)}) copy-start(f32[1,256]{1,0:T(1,128)S(1)} %get-tuple-element.112) | copy-start | bytes 3076
  15.4 34.3 %copy-start.25 = (f32[1,256]{1,0:T(1,128)}, f32[1,256]{1,0:T(1,128)S(1)}, u32[]{:S(2)}) copy-start(f32[1,256]{1,0:T(1,128)S(1)} %get-tuple-element.113) | copy-start | bytes 3076
  15.5 34.3 %copy-start.27 = (f32[1,256]{1,0:T(1,128)}, f32[1,256]{1,0:T(1,128)S(1)}, u32[]{:S(2)}) copy-start(f32[1,256]{1,0:T(1,128)S(1)} %get-tuple-element.114) | copy-start | bytes 3076
  16.1 33.7 %copy-start.83 = (pred[256]{0:T(512)(128)(4,1)}, pred[256]{0:T(512)(128)(4,1)S(1)}, u32[]{:S(2)}) copy-start(pred[256]{0:T(512)(128)(4,1)S(1)} %get-tuple-element.131) | copy-start | bytes 772
  16.1 33.7 %copy-start.85 = (pred[256]{0:T(512)(128)(4,1)}, pred[256]{0:T(512)(128)(4,1)S(1)}, u32[]{:S(2)}) copy-start(pred[256]{0:T(512)(128)(4,1)S(1)} %get-tuple-element.132) | copy-start | bytes 772
  16.8 33.0 %copy-start.57 = (pred[256]{0:T(512)(128)(4,1)}, pred[256]{0:T(512)(128)(4,1)S(1)}, u32[]{:S(2)}) copy-start(pred[256]{0:T(512)(128)(4,1)S(1)} %get-tuple-element.228) | copy-start | bytes 772
  77.2 26.0 %copy-start.3 = (bf16[256,256]{1,0:T(8,128)(2,1)S(1)}, bf16[256,256]{1,0:T(8,128)(2,1)}, u32[]{:S(2)}) copy-start(bf16[256,256]{1,0:T(8,128)(2,1)} %get-tuple-element.71) | copy-start | bytes 393220
  77.2 26.0 %copy-start.4 = (bf16[256,256]{1,0:T(8,128)(2,1)S(1)}, bf16[256,256]{1,0:T(8,128)(2,1)}, u32[]{:S(2)}) copy-start(bf16[256,256]{1,0:T(8,128)(2,1)} %get-tuple-element.72) | copy-start | bytes 393220
  217.5 2.6 copy-start.6
  217.5 2.6 copy-start.10
  217.5 2.6 copy-start.12
  217.5 2.6 copy-start.14
  (97 other events, 139.7 us)
Sparse Core Ops, SparseCore 0:
  62.5 476.5 all-reduce.3
where the time goes:
time: 550 us; the launch traced here: 549 us
  waiting for transfers between devices  311 us (57%)
  blocking collectives  160 us (29%)
  other arithmetic  38.9 us (7%)
  between operations  22.3 us (4%)
  local copies, waits for them, and re-layouts  9.01 us (2%)
  matrix products  7.31 us (1%)
    psum x1, waiting for transfers between devices, per_device(): lax.psum((grad_up, grad_down, grad_kernel, grad_gain), ('dp', 'seq'))  311 us
    psum x1, blocking collectives, per_device(): lax.psum((grad_up, grad_down, grad_kernel, grad_gain), ('dp', 'seq'))  106 us
    all_gather x1, blocking collectives, per_device(): arrived = lax.all_gather(tail_rows[None], 'seq', axis=0, tiled=True)  28.7 us
    all_gather x1, blocking collectives, per_device(): lax.all_gather(head_rows[None].astype(jnp.bfloat16), 'seq', axis=0, tiled...  25.3 us
    reduce_sum x8, other arithmetic, per_device(): jnp.sum(jnp.where((offset <= depth)[:, None], grad_conv_out * window, 0.0...  12.6 us
  transfers between devices with their start and end apart: 1, of which 1 were waited for; matrix products, arithmetic and copies ran while one was open for 5% of the time, Pallas kernels for 0%

commit v1 on v0

v1 whole, which is shorter than its diff:
```python
import math

import jax
import jax.numpy as jnp
from jax import lax
from jax.experimental import pallas as pl
from jax.experimental.pallas import tpu as pltpu
from jax.sharding import PartitionSpec as P

MESH = pl.DeviceIdType.MESH
F32 = jnp.float32
BF16 = jnp.bfloat16

EPS = 1e-05
C = 256
HID = 1024
K = 51
ROWS = 256
TRACES = 8
HALO = 64
BLK = 64
NZ, NSEQ, NQ = 16, 32, 16
CH = 4
FACTOR = 1.0 / math.sqrt(NZ * NSEQ * ROWS)
GELU_C = math.sqrt(2.0 / math.pi)
GELU_A = 0.044715


def dot(a, b, ca, cb):
    return lax.dot_general(a, b, (((ca,), (cb,)), ((), ())), preferred_element_type=F32)


def remote(src, dst, send, recv, dev):
    return pltpu.make_async_remote_copy(
        src_ref=src, dst_ref=dst, send_sem=send, recv_sem=recv, device_id=dev, device_id_type=MESH
    )


def loop(lo, hi, body):
    def step(i, carry):
        body(i)
        return carry

    lax.fori_loop(lo, hi, step, 0)


def kernel(
    lengths, placed, x_ref, dy_ref, w_ref, gain_ref, up_hbm, down_hbm,
    out_ref, gin_ref, gk_ref, gg_ref, gu_hbm, gd_hbm,
    up_v, down_v, gath0, gath1, send_b, recv0, recv1, head, ext, gext, dep, rem_, normed_s, istd_s, scaled_s,
    gn_s, oacc_s, own, outbound, sib, tsum, r1, zs, r2, a1, fin, kp, kb, rk, rz, kf,
    ld_sem, a_s, a_r, b_s, b_r, c_s, c_r, p_s, p_r, z_s, z_r, y_s, y_r, q_s, q_r, f_s, f_r,
    k_s, k_r, kz_s, kz_r, kf_s, kf_r, st_sem,
):
    z = lax.axis_index("dp")
    s = lax.axis_index("seq")
    core = lax.rem(s, 2)
    q = lax.div(s, 2)
    yy = lax.rem(q, 4)
    xx = lax.div(q, 4)
    g = xx * 2 + core
    sibling = (z, q * 2 + 1 - core)
    gath, recv = (gath0, gath1), (recv0, recv1)

    bar = pltpu.get_barrier_semaphore()
    loop(1, NSEQ, lambda i: pl.semaphore_signal(
        bar, inc=1, device_id=(z, lax.rem(s + i, NSEQ)), device_id_type=MESH))
    loop(1, NZ, lambda i: pl.semaphore_signal(
        bar, inc=1, device_id=(lax.rem(z + i, NZ), s), device_id_type=MESH))
    loads = [
        pltpu.make_async_copy(up_hbm, up_v, ld_sem.at[0]),
        pltpu.make_async_copy(down_hbm, down_v, ld_sem.at[1]),
    ]
    for copy in loads:
        copy.start()

    def target(i):
        gt = lax.rem(g + i, 8)
        return (lax.div(gt, 2) * 4 + yy) * 2 + lax.rem(gt, 2)

    targets = [target(i) for i in range(8)]
    at = [placed[0, t] for t in targets]

    def look(k, found):
        p = placed[0, k]
        return tuple(
            jnp.where(p == at[i % 8] + (-1 if i < 8 else 1), k, f) for i, f in enumerate(found)
        )

    found = lax.fori_loop(0, NSEQ, look, (jnp.int32(0),) * 16)
    before, after = found[:8], found[8:]

    def y_of(slot):
        return lax.rem(lax.div(slot, 2), 4)

    def g_of(slot):
        return lax.div(slot, 8) * 2 + lax.rem(slot, 2)

    pl.semaphore_wait(bar, NSEQ - 1 + NZ - 1)

    def phase_a(d, src):
        def copy(i):
            peer = (xx * 4 + lax.rem(yy + i, 4)) * 2 + core
            return remote(src, gath[d].at[yy], a_s.at[d, i], a_r.at[d, i], (z, peer))

        for i in range(1, 4):
            copy(i).start()
        gath[d][yy] = src[...]

    def phase_a_wait(d):
        for i in range(1, 4):
            slot = gath[d].at[lax.rem(yy + 4 - i, 4)]
            remote(slot, slot, a_s.at[d, i], a_r.at[d, i], sibling).wait_recv()

    def phase_b(d, source):
        for i in range(1, 8):
            send_b[d, i] = gath[d][y_of(source[i])]
            remote(send_b.at[d, i], recv[d].at[g], b_s.at[d, i], b_r.at[d, i], (z, targets[i])).start()
        recv[d][g] = gath[d][y_of(source[0])]

    def phase_b_wait(d, source):
        for i in range(1, 8):
            slot = recv[d].at[lax.rem(g + 8 - i, 8)]
            remote(slot, slot, b_s.at[d, i], b_r.at[d, i], sibling).wait_recv()
        return recv[d][g_of(source[0])].astype(F32)

    tail = x_ref.at[pl.ds(ROWS - HALO, HALO), :]
    phase_a(0, tail)

    pos = at[0] * ROWS + lax.broadcasted_iota(jnp.int32, (ROWS, 128), 0)
    ends, end = [], jnp.int32(0)
    for i in range(TRACES):
        end = end + lengths[0, i]
        ends.append(end)
    start = jnp.zeros((ROWS, 128), jnp.int32)
    for e in ends:
        start = jnp.where(e <= pos, e, start)
    dep[...] = pos - start
    stop = jnp.zeros((ROWS, 128), jnp.int32)
    for e in reversed(ends):
        stop = jnp.where(e > pos, e, stop)
    rem_[...] = stop - 1 - pos

    for hf in range(2):
        ext[hf, HALO:, :] = x_ref[:, hf * 128:(hf + 1) * 128].astype(F32)

    phase_a_wait(0)
    phase_b(0, before)

    def depthwise(src, base, sign, mask_ref, r0):
        m = mask_ref[r0:r0 + BLK, :]
        acc = [jnp.zeros((BLK, 128), F32) for _ in range(2)]
        for j in range(K):
            lo = base + r0 + sign * j
            inside = m >= j
            for hf in range(2):
                win = src[hf, lo:lo + BLK, :] * w_ref[j:j + 1, hf * 128:(hf + 1) * 128]
                acc[hf] = acc[hf] + jnp.where(inside, win, 0.0)
        return acc

    def forward_block(r0):
        a0, a1_ = depthwise(ext, HALO, -1, dep, r0)
        mean = (jnp.sum(a0, axis=1, keepdims=True) + jnp.sum(a1_, axis=1, keepdims=True)) * (1.0 / C)
        a0, a1_ = a0 - mean, a1_ - mean
        var = (jnp.sum(a0 * a0, axis=1, keepdims=True) + jnp.sum(a1_ * a1_, axis=1, keepdims=True)) * (1.0 / C)
        inv = lax.rsqrt(var + EPS)
        istd_s[r0:r0 + BLK, :] = jnp.broadcast_to(inv, (BLK, 128))
        for hf, a in enumerate((a0, a1_)):
            cols = slice(hf * 128, (hf + 1) * 128)
            n = a * inv
            normed_s[r0:r0 + BLK, cols] = n
            scaled_s[r0:r0 + BLK, cols] = (n * gain_ref[0:1, cols]).astype(BF16)

    for r0 in range(BLK, ROWS, BLK):
        forward_block(r0)
    halo = phase_b_wait(0, before)
    for hf in range(2):
        ext[hf, :HALO, :] = halo[:, hf * 128:(hf + 1) * 128]
    forward_block(0)

    for copy in loads:
        copy.wait()

    def chip(k):
        qp = lax.rem(xx + lax.div(k, 4), 4) * 4 + lax.rem(yy + lax.rem(k, 4), 4)
        return qp

    def chip_back(k):
        return lax.rem(xx + 4 - lax.div(k, 4), 4) * 4 + lax.rem(yy + 4 - lax.rem(k, 4), 4)

    def rows16(i):
        return pl.ds(pl.multiple_of(i * 16, 16), 16)

    def mlp_chunk(h):
        cols = slice(h * 256, (h + 1) * 256)
        up_c = up_v[:, cols]
        down_c = down_v[cols, :]
        hid = dot(scaled_s[...], up_c, 1, 0)
        gact = dot(dy_ref[...], down_c, 1, 1)
        h2 = hid * hid
        th = jnp.tanh(hid * (GELU_C + (GELU_C * GELU_A) * h2))
        h1 = 0.5 + 0.5 * th
        act = hid * h1
        slope = h1 + act * (1.0 - th) * (GELU_C + (3.0 * GELU_C * GELU_A) * h2)
        act = act.astype(BF16)
        gh = (gact * slope).astype(BF16)
        o = dot(act, down_c, 1, 0)
        n = dot(gh, up_c, 1, 1)
        if h == 0:
            oacc_s[...] = o
            gn_s[...] = n
        else:
            oacc_s[...] += o
            gn_s[...] += n
        gdown = dot(act, dy_ref[...], 0, 0)
        gup = dot(scaled_s[...], gh, 0, 0)
        first = core == 0
        own[h] = jnp.where(first, gdown, gup)
        outbound[h] = jnp.where(first, gup, gdown).astype(BF16)
        remote(outbound.at[h], sib.at[h], c_s.at[h], c_r.at[h], sibling).start()

    def pair_stage(h):
        remote(sib.at[h], sib.at[h], c_s.at[h], c_r.at[h], sibling).wait_recv()
        tsum[h] = (own[h] + sib[h].astype(F32)).astype(BF16)

        def send(k):
            qp = chip(k)
            remote(tsum.at[h, rows16(qp), :], r1.at[h, k], p_s.at[h, k], p_r.at[h, k],
                   (z, qp * 2 + core)).start()

        loop(1, NQ, send)

    for h in range(CH):
        mlp_chunk(h)
        if h:
            pair_stage(h - 1)
    out_ref[...] = (x_ref[...].astype(F32) + oacc_s[...]).astype(BF16)
    pair_stage(CH - 1)

    ggain = jnp.zeros((1, C), F32)
    for r0 in range(0, ROWS, BLK):
        gn = gn_s[r0:r0 + BLK, :]
        nm = normed_s[r0:r0 + BLK, :]
        ggain = ggain + jnp.sum(gn * nm, axis=0, keepdims=True)
        qv = gn * gain_ref[...]
        m1 = jnp.sum(qv, axis=1, keepdims=True) * (1.0 / C)
        m2 = jnp.sum(qv * nm, axis=1, keepdims=True) * (1.0 / C)
        t = qv - m1 - nm * m2
        for hf in range(2):
            gext[hf, r0:r0 + BLK, :] = t[:, hf * 128:(hf + 1) * 128] * istd_s[r0:r0 + BLK, :]
    for hf in range(2):
        head[:, hf * 128:(hf + 1) * 128] = gext[hf, :HALO, :].astype(BF16)
    phase_a(1, head)

    for r0 in range(0, ROWS, BLK):
        m = dep[r0:r0 + BLK, :]
        gc = [gext[hf, r0:r0 + BLK, :] for hf in range(2)]
        for j in range(K):
            lo = HALO + r0 - j
            inside = m >= j
            for hf in range(2):
                v = jnp.where(inside, gc[hf] * ext[hf, lo:lo + BLK, :], 0.0)
                part = jnp.sum(v.reshape(BLK // 8, 8, 128), axis=0)
                if r0 == 0:
                    kp[hf, j] = part
                else:
                    kp[hf, j] += part
    for hf in range(2):
        taps = jnp.sum(kp[hf], axis=1)
        taps = jnp.concatenate(
            [taps, ggain[:, hf * 128:(hf + 1) * 128], jnp.zeros((64 - K - 1, 128), F32)], axis=0)
        for r in range(8):
            kb[2 * r + hf] = taps[r * 8:r * 8 + 8, :]

    def send_k(i):
        p = lax.rem(q + i, NQ)
        return remote(kb.at[p], rk.at[s], k_s.at[i], k_r.at[s], (z, p * 2))

    loop(1, NQ, lambda i: send_k(i).start())

    @pl.when(core == 1)
    def _():
        send_k(0).start()

    for h in range(CH):
        def got(k, h=h):
            remote(r1.at[h, k], r1.at[h, k], p_s.at[h, k], p_r.at[h, k], sibling).wait_recv()

        loop(1, NQ, got)
        acc = tsum[h, rows16(q), :].astype(F32)
        for k in range(1, NQ):
            acc = acc + r1[h, k].astype(F32)
        for rh in range(2):
            for hf in range(2):
                zs[h * 4 + rh * 2 + hf] = acc[rh * 8:rh * 8 + 8, hf * 128:(hf + 1) * 128]

    def send_z(i):
        zp = lax.rem(z + i, NZ)
        return remote(zs.at[zp], r2.at[i], z_s.at[i], z_r.at[i], (zp, s))

    loop(1, NZ, lambda i: send_z(i).start())

    phase_a_wait(1)
    phase_b(1, after)

    def back_block(r0):
        acc = depthwise(gext, 0, 1, rem_, r0)
        for hf in range(2):
            cols = slice(hf * 128, (hf + 1) * 128)
            gin_ref[r0:r0 + BLK, cols] = (dy_ref[r0:r0 + BLK, cols].astype(F32) + acc[hf]).astype(BF16)

    back_block(0)

    loop(1, NZ, lambda i: send_z(i).wait_recv())
    total = zs[z]
    for i in range(1, NZ):
        total = total + r2[i]
    a1[z] = total * FACTOR

    def send_y(i):
        return remote(a1.at[z], a1.at[z], y_s.at[i], y_r.at[i], (lax.rem(z + i, NZ), s))

    loop(1, NZ, lambda i: send_y(i).start())

    @pl.when(core == 0)
    def _():
        def got(i):
            sp = lax.rem(s + i, NSEQ)
            remote(rk.at[sp], rk.at[sp], k_s.at[0], k_r.at[sp], sibling).wait_recv()

        loop(1, NSEQ, got)
        rk[s] = kb[q]
        acc = rk[0]
        for i in range(1, NSEQ):
            acc = acc + rk[i]
        rz[z] = acc
        loop(1, NZ, lambda i: remote(
            rz.at[z], rz.at[z], kz_s.at[i], kz_r.at[i], (lax.rem(z + i, NZ), s)).start())

    back_block(64)

    def got_y(i):
        slot = a1.at[lax.rem(z + NZ - i, NZ)]
        remote(slot, slot, y_s.at[i], y_r.at[i], sibling).wait_recv()

    loop(1, NZ, got_y)
    for h in range(CH):
        top = jnp.concatenate([a1[4 * h], a1[4 * h + 1]], axis=1)
        bottom = jnp.concatenate([a1[4 * h + 2], a1[4 * h + 3]], axis=1)
        fin[core, h, rows16(q), :] = jnp.concatenate([top, bottom], axis=0).astype(BF16)

    def piece(i):
        return fin.at[core, :, rows16(i), :]

    def send_q(k):
        return remote(piece(q), piece(q), q_s.at[k], q_r.at[k], (z, chip(k) * 2 + core))

    def send_f(k):
        return remote(piece(chip_back(k)), piece(chip_back(k)), f_s.at[k], f_r.at[k], sibling)

    loop(1, NQ, lambda k: send_q(k).start())
    send_f(jnp.int32(0)).start()

    back_block(128)
    halo_g = phase_b_wait(1, after)
    for hf in range(2):
        gext[hf, ROWS:, :] = halo_g[:, hf * 128:(hf + 1) * 128]
    back_block(192)

    @pl.when(core == 0)
    def _():
        def got(i):
            slot = rz.at[lax.rem(z + NZ - i, NZ)]
            remote(slot, slot, kz_s.at[i], kz_r.at[i], sibling).wait_recv()

        loop(1, NZ, got)
        acc = rz[0]
        for i in range(1, NZ):
            acc = acc + rz[i]
        kf[q] = acc * FACTOR
        loop(1, NSEQ, lambda i: remote(
            kf.at[q], kf.at[q], kf_s.at[i], kf_r.at[q], (z, lax.rem(s + i, NSEQ))).start())

    def forward(k):
        slot = piece(chip_back(k))
        remote(slot, slot, q_s.at[k], q_r.at[k], sibling).wait_recv()
        send_f(k).start()

    loop(1, NQ, forward)

    def got_kf(i):
        slot = lax.rem(q + i, NQ)
        remote(kf.at[slot], kf.at[slot], kf_s.at[0], kf_r.at[slot], sibling).wait_recv()

    loop(1, NQ, got_kf)

    @pl.when(core == 1)
    def _():
        got_kf(0)

    for hf in range(2):
        cols = slice(hf * 128, (hf + 1) * 128)
        taps = jnp.concatenate([kf[2 * r + hf] for r in range(8)], axis=0)
        gk_ref[:, cols] = taps[:K, :].astype(BF16)
        gg_ref[:, cols] = taps[K:K + 1, :].astype(BF16)

    def got_f(k):
        slot = fin.at[1 - core, :, rows16(chip_back(k)), :]
        remote(slot, slot, f_s.at[k], f_r.at[k], sibling).wait_recv()

    loop(0, NQ, got_f)
    stores = []
    for h in range(CH):
        cols = pl.ds(h * 256, 256)
        stores.append(pltpu.make_async_copy(fin.at[0, h], gd_hbm.at[cols, :], st_sem.at[h]))
        stores.append(pltpu.make_async_copy(fin.at[1, h], gu_hbm.at[:, cols], st_sem.at[CH + h]))
    for copy in stores:
        copy.start()

    for d, src in ((0, tail), (1, head)):
        for i in range(1, 4):
            remote(src, src, a_s.at[d, i], a_r.at[d, i], sibling).wait_send()
        for i in range(1, 8):
            remote(send_b.at[d, i], send_b.at[d, i], b_s.at[d, i], b_r.at[d, i], sibling).wait_send()
    for h in range(CH):
        remote(outbound.at[h], outbound.at[h], c_s.at[h], c_r.at[h], sibling).wait_send()

        def sent(k, h=h):
            slot = tsum.at[h, rows16(chip(k)), :]
            remote(slot, slot, p_s.at[h, k], p_r.at[h, k], sibling).wait_send()

        loop(1, NQ, sent)
    loop(1, NZ, lambda i: send_z(i).wait_send())
    loop(1, NZ, lambda i: send_y(i).wait_send())
    loop(1, NQ, lambda k: send_q(k).wait_send())
    loop(0, NQ, lambda k: send_f(k).wait_send())
    loop(1, NQ, lambda i: send_k(i).wait_send())

    @pl.when(core == 1)
    def _():
        send_k(0).wait_send()

    @pl.when(core == 0)
    def _():
        loop(1, NZ, lambda i: remote(
            rz.at[z], rz.at[z], kz_s.at[i], kz_r.at[i], sibling).wait_send())
        loop(1, NSEQ, lambda i: remote(
            kf.at[q], kf.at[q], kf_s.at[i], kf_r.at[q], sibling).wait_send())

    for copy in stores:
        copy.wait()


def per_device(inputs, cotangent, lengths, placed, conv_weight, norm_gain, up_weight, down_weight):
    vm = pl.BlockSpec(memory_space=pltpu.VMEM)
    sm = pl.BlockSpec(memory_space=pltpu.SMEM)
    hb = pl.BlockSpec(memory_space=pl.ANY)
    V, D = pltpu.VMEM, pltpu.SemaphoreType.DMA
    out, gin, gk, gg, gu, gd = pl.pallas_call(
        kernel,
        out_shape=(
            jax.ShapeDtypeStruct((ROWS, C), BF16),
            jax.ShapeDtypeStruct((ROWS, C), BF16),
            jax.ShapeDtypeStruct((K, C), BF16),
            jax.ShapeDtypeStruct((1, C), BF16),
            jax.ShapeDtypeStruct((C, HID), BF16),
            jax.ShapeDtypeStruct((HID, C), BF16),
        ),
        in_specs=[sm, sm, vm, vm, vm, vm, hb, hb],
        out_specs=(vm, vm, vm, vm, hb, hb),
        scratch_shapes=[
            V((C, HID), BF16), V((HID, C), BF16),
            V((4, HALO, C), BF16), V((4, HALO, C), BF16), V((2, 8, HALO, C), BF16),
            V((8, HALO, C), BF16), V((8, HALO, C), BF16),
            V((HALO, C), BF16),
            V((2, HALO + ROWS, 128), F32), V((2, ROWS + HALO, 128), F32),
            V((ROWS, 128), jnp.int32), V((ROWS, 128), jnp.int32),
            V((ROWS, C), F32), V((ROWS, 128), F32), V((ROWS, C), BF16),
            V((ROWS, C), F32), V((ROWS, C), F32),
            V((CH, 256, 256), F32), V((CH, 256, 256), BF16), V((CH, 256, 256), BF16), V((CH, 256, 256), BF16),
            V((CH, NQ, 16, 256), BF16),
            V((NZ, 8, 128), F32), V((NZ, 8, 128), F32), V((NZ, 8, 128), F32),
            V((2, CH, 256, 256), BF16),
            V((2, K, 8, 128), F32), V((NQ, 8, 128), F32), V((NSEQ, 8, 128), F32),
            V((NZ, 8, 128), F32), V((NQ, 8, 128), F32),
            D((2,)), D((2, 4)), D((2, 4)), D((2, 8)), D((2, 8)), D((CH,)), D((CH,)),
            D((CH, NQ)), D((CH, NQ)), D((NZ,)), D((NZ,)), D((NZ,)), D((NZ,)), D((NQ,)), D((NQ,)),
            D((NQ,)), D((NQ,)), D((NQ,)), D((NSEQ,)), D((NZ,)), D((NZ,)), D((NSEQ,)), D((NQ,)), D((2 * CH,)),
        ],
        compiler_params=pltpu.CompilerParams(
            collective_id=0, has_side_effects=True, vmem_limit_bytes=48 * 2**20
        ),
    )(
        lengths, placed, inputs.reshape(ROWS, C), cotangent.reshape(ROWS, C), conv_weight,
        norm_gain.reshape(1, C), up_weight, down_weight,
    )
    return (
        out.reshape(inputs.shape), gin.reshape(inputs.shape), gk, gg.reshape(C), gu, gd,
    )


def solution(mesh):
    tok = P("dp", "seq", None, None)
    return jax.shard_map(
        per_device,
        mesh=mesh,
        in_specs=(tok, tok, P("dp", None), P("dp", None), P(), P(), P(), P()),
        out_specs=(tok, tok, P(), P(), P(), P()),
        check_vma=False,
    )
```

time: 550 us -> 81.7 us (0.15)
  waiting for transfers between devices: 311 us -> 0 us
  blocking collectives: 160 us -> 0 us
  Pallas kernels: 0 us -> 71.3 us
  other arithmetic: 38.9 us -> 0.53 us
  between operations: 22.3 us -> 0.68 us
  matrix products: 7.31 us -> 0 us
    psum x1 -> x0, waiting for transfers between devices: 311 us -> none  [per_device(): lax.psum((grad_up, grad_down, grad_kernel, grad_gain), ('dp', 'seq'))]
    psum x1 -> x0, blocking collectives: 106 us -> none  [per_device(): lax.psum((grad_up, grad_down, grad_kernel, grad_gain), ('dp', 'seq'))]
    pallas_call x0 -> x1, Pallas kernels: none -> 71.3 us  [per_device(): pl.pallas_call(kernel, out_shape=(jax.ShapeDtypeStruct((ROWS, C), BF16),...]
    all_gather x2 -> x0, blocking collectives: 54 us -> none  [the longest x1 28.7 us: per_device(): arrived = lax.all_gather(tail_rows[None], 'seq', axis=0, tiled=True)]
    reduce_sum x13 -> x0, other arithmetic: 22.4 us -> none  [the longest x8 12.6 us: per_device(): jnp.sum(jnp.where((offset <= depth)[:, None], grad_conv_out * window, 0.0...]
    dot_general x6 -> x0, matrix products: 7.31 us -> none  [the longest x2 2.99 us: contract_rows(): lax.dot_general(left, right, (((0,), (0,)), ((), ())), preferred_element_...]
    reshape x1 -> x0, other arithmetic: 7.29 us -> none  [per_device(): grad_series.reshape(inputs.shape)]
  transfers between devices with their start and end apart: 1 -> 0, of which waited for: 1 -> 0; matrix products, arithmetic and copies ran while one was open for 5% -> 0% of each run, Pallas kernels for 0% -> 0%
where the time goes in v1:
time: 81.7 us; the launch traced here: 81.4 us
  Pallas kernels  71.3 us (87%)
  local copies, waits for them, and re-layouts  8.89 us (11%)
    pallas_call x1, Pallas kernels, per_device(): pl.pallas_call(kernel, out_shape=(jax.ShapeDtypeStruct((ROWS, C), BF16),...  71.3 us
    unnamed x21, local copies, waits for them, and re-layouts  8.89 us

profile of v1, /device:TPU:1, one launch (start us, length us, event | category | flops | bytes accessed | tf_op | source)
XLA Modules:
  0.0 81.4 jit_solution(5779781140524671295)
XLA Ops:
  0.6 0.0 copy-start.7
  0.6 0.0 copy-start.5
  0.7 0.0 copy-start.6
  0.7 0.6 copy-done.7
  1.3 0.0 copy-done.5
  1.3 0.0 copy-done.6
  1.3 0.0 copy-start
  1.3 1.0 %copy-done = bf16[256,1024]{1,0:T(8,128)(2,1)S(1)} copy-done((bf16[256,1024]{1,0:T(8,128)(2,1)S(1)}, bf16[256,1024]{1,0:T(8,128)(2,1)}, u32[]{:S(2)}) %copy-start) | copy-done | bytes 524312
  2.4 0.0 copy-start.1
  2.4 1.0 %copy-done.1 = bf16[1024,256]{1,0:T(8,128)(2,1)S(1)} copy-done((bf16[1024,256]{1,0:T(8,128)(2,1)S(1)}, bf16[1024,256]{1,0:T(8,128)(2,1)}, u32[]{:S(2)}) %copy-start.1) | copy-done | bytes 524312
  3.4 0.0 copy-start.2
  3.4 0.9 %copy-done.2 = bf16[1,1,256,256]{3,2,1,0:T(8,128)(2,1)S(1)} copy-done((bf16[1,1,256,256]{3,2,1,0:T(8,128)(2,1)S(1)}, bf16[1,1,256,256]{3,2,1,0:T(8,128)(2,1)}, u32[]{:S(2)}) %copy-start.2) | copy-done | bytes 131096
  4.3 0.0 copy-start.3
  4.3 0.9 %copy-done.3 = bf16[1,1,256,256]{3,2,1,0:T(8,128)(2,1)S(1)} copy-done((bf16[1,1,256,256]{3,2,1,0:T(8,128)(2,1)S(1)}, bf16[1,1,256,256]{3,2,1,0:T(8,128)(2,1)}, u32[]{:S(2)}) %copy-start.3) | copy-done | bytes 131096
  5.2 0.0 copy-start.4
  5.2 0.8 %copy-done.4 = f32[51,256]{1,0:T(8,128)S(1)} copy-done((f32[51,256]{1,0:T(8,128)S(1)}, f32[51,256]{1,0:T(8,128)}, u32[]{:S(2)}) %copy-start.4) | copy-done | bytes 52248
  6.0 71.3 %shard_map.127 = (bf16[256,256]{1,0:T(8,128)(2,1)S(1)}, bf16[256,256]{1,0:T(8,128)(2,1)S(1)}, bf16[51,256]{1,0:T(8,128)(2,1)S(1)}, bf16[1,256]{1,0:T(2,128)(2,1)...) custom-call(s32[1,8]{1,0:T(1,128)S(1)} %copy-done.6, s32[1,32]{1,0:T(1,128)S(1)} %copy-done.7, ...), custom_call_target="tpu_custom_call" | custom-call | tf_op jit(solution)/shard_map/pallas_call | solution.py:459
  77.4 0.5 reduce
  77.9 0.7 copy.19
  78.6 0.7 copy.20
  79.2 0.6 copy.21
  79.8 0.8 copy.22
  80.6 0.8 copy.23
Async XLA Ops:
  0.6 0.7 copy-start.7
  0.6 0.7 copy-start.5
  0.7 0.7 copy-start.6
  1.3 1.0 %copy-start = (bf16[256,1024]{1,0:T(8,128)(2,1)S(1)}, bf16[256,1024]{1,0:T(8,128)(2,1)}, u32[]{:S(2)}) copy-start(bf16[256,1024]{1,0:T(8,128)(2,1)} %up_hbm.1) | copy-start | bytes 1572868
  2.4 1.0 %copy-start.1 = (bf16[1024,256]{1,0:T(8,128)(2,1)S(1)}, bf16[1024,256]{1,0:T(8,128)(2,1)}, u32[]{:S(2)}) copy-start(bf16[1024,256]{1,0:T(8,128)(2,1)} %down_hbm.1) | copy-start | bytes 1572868
  3.4 0.9 %copy-start.2 = (bf16[1,1,256,256]{3,2,1,0:T(8,128)(2,1)S(1)}, bf16[1,1,256,256]{3,2,1,0:T(8,128)(2,1)}, u32[]{:S(2)}) copy-start(bf16[1,1,256,256]{3,2,1,0:T(8,128)(2,1)} %param.8) | copy-start | bytes 393220
  4.3 0.9 %copy-start.3 = (bf16[1,1,256,256]{3,2,1,0:T(8,128)(2,1)S(1)}, bf16[1,1,256,256]{3,2,1,0:T(8,128)(2,1)}, u32[]{:S(2)}) copy-start(bf16[1,1,256,256]{3,2,1,0:T(8,128)(2,1)} %param.9) | copy-start | bytes 393220
  5.2 0.8 %copy-start.4 = (f32[51,256]{1,0:T(8,128)S(1)}, f32[51,256]{1,0:T(8,128)}, u32[]{:S(2)}) copy-start(f32[51,256]{1,0:T(8,128)} %w_ref.1) | copy-start | bytes 156676

commit v2 on v1

v2 whole, which is shorter than its diff:
```python
import math

import jax
import jax.numpy as jnp
from jax import lax
from jax.experimental import pallas as pl
from jax.experimental.pallas import tpu as pltpu
from jax.sharding import PartitionSpec as P

MESH = pl.DeviceIdType.MESH
F32 = jnp.float32
BF16 = jnp.bfloat16

EPS = 1e-05
C = 256
HID = 1024
K = 51
ROWS = 256
TRACES = 8
HALO = 64
BLK = 64
NZ, NSEQ, NQ = 16, 32, 16
VM_BYTES = 60 * 2**20
CH = 4
FACTOR = 1.0 / math.sqrt(NZ * NSEQ * ROWS)
GELU_C = math.sqrt(2.0 / math.pi)
GELU_A = 0.044715
FAR_Z = (8, 7, 9, 6, 10, 5, 11, 4, 12, 3, 13, 2, 14, 1, 15)


def dot(a, b, ca, cb):
    return lax.dot_general(a, b, (((ca,), (cb,)), ((), ())), preferred_element_type=F32)


def remote(src, dst, send, recv, dev):
    return pltpu.make_async_remote_copy(
        src_ref=src, dst_ref=dst, send_sem=send, recv_sem=recv, device_id=dev, device_id_type=MESH
    )


def loop(lo, hi, body):
    def step(i, carry):
        body(i)
        return carry

    lax.fori_loop(lo, hi, step, 0)


def kernel(
    lengths, placed, x_hbm, dy_hbm, w_hbm, gain_hbm, up_hbm, down_hbm,
    out_hbm, gin_hbm, gk_hbm, gg_hbm, gu_hbm, gd_hbm,
    out_ref, gin_ref, gk_ref, gg_ref, fin, x_ref, dy_ref, w_ref, gain_ref, up_v, down_v,
    gath0, gath1, send_b, recv0, recv1, head, ext, gext, dep, rem_, normed_s, istd_s, scaled_s,
    gn_s, oacc_s, own, other, outbound, sib, tsum, r1, zs, r2, a1, kp, gp, kb, rk, rz, kf,
    ld_sem, a_s, a_r, b_s, b_r, c_s, c_r, p_s, p_r, z_s, z_r, y_s, y_r, q_s, q_r, f_s, f_r,
    k_s, k_r, kz_s, kz_r, kf_s, kf_r, st_sem,
):
    z = lax.axis_index("dp")
    s = lax.axis_index("seq")
    core = lax.rem(s, 2)
    q = lax.div(s, 2)
    yy = lax.rem(q, 4)
    xx = lax.div(q, 4)
    g = xx * 2 + core
    gz = lax.div(z, 4)
    sibling = (z, q * 2 + 1 - core)
    gath, recv = (gath0, gath1), (recv0, recv1)

    bar = pltpu.get_barrier_semaphore()
    for i in FAR_Z:
        pl.semaphore_signal(bar, inc=1, device_id=(lax.rem(z + i, NZ), s), device_id_type=MESH)
    loop(0, NSEQ - 1, lambda i: pl.semaphore_signal(
        bar, inc=1, device_id=(z, lax.rem(s + 1 + lax.rem(i + 19, NSEQ - 1), NSEQ)), device_id_type=MESH))
    loads = [
        pltpu.make_async_copy(src, dst, ld_sem.at[i])
        for i, (src, dst) in enumerate((
            (x_hbm, x_ref), (w_hbm, w_ref), (gain_hbm, gain_ref),
            (dy_hbm, dy_ref), (up_hbm, up_v), (down_hbm, down_v)))
    ]
    for copy in loads:
        copy.start()

    def target(i):
        gt = lax.rem(g + i, 8)
        return (lax.div(gt, 2) * 4 + yy) * 2 + lax.rem(gt, 2)

    targets = [target(i) for i in range(8)]
    at = [placed[0, t] for t in targets]

    def look(k, found):
        p = placed[0, k]
        return tuple(
            jnp.where(p == at[i % 8] + (-1 if i < 8 else 1), k, f) for i, f in enumerate(found)
        )

    found = lax.fori_loop(0, NSEQ, look, (jnp.int32(0),) * 16)
    before, after = found[:8], found[8:]

    def y_of(slot):
        return lax.rem(lax.div(slot, 2), 4)

    def g_of(slot):
        return lax.div(slot, 8) * 2 + lax.rem(slot, 2)

    pos = at[0] * ROWS + lax.broadcasted_iota(jnp.int32, (ROWS, 128), 0)
    ends, end = [], jnp.int32(0)
    for i in range(TRACES):
        end = end + lengths[0, i]
        ends.append(end)
    start = jnp.zeros((ROWS, 128), jnp.int32)
    for e in ends:
        start = jnp.where(e <= pos, e, start)
    dep[...] = pos - start
    stop = jnp.zeros((ROWS, 128), jnp.int32)
    for e in reversed(ends):
        stop = jnp.where(e > pos, e, stop)
    rem_[...] = stop - 1 - pos
    loads[0].wait()
    for hf in range(2):
        ext[hf, HALO:, :] = x_ref[:, hf * 128:(hf + 1) * 128].astype(F32)
    loads[1].wait()
    loads[2].wait()

    def phase_a(d, src):
        for i in range(1, 4):
            peer = (xx * 4 + lax.rem(yy + i, 4)) * 2 + core
            remote(src, gath[d].at[yy], a_s.at[d, i], a_r.at[d, i], (z, peer)).start()
        gath[d][yy] = src[...]

    def phase_a_wait(d):
        for i in range(1, 4):
            slot = gath[d].at[lax.rem(yy + 4 - i, 4)]
            remote(slot, slot, a_s.at[d, i], a_r.at[d, i], sibling).wait_recv()

    def phase_b(d, source):
        for i in (4, 5, 3, 2, 6, 7, 1):
            send_b[d, i] = gath[d][y_of(source[i])]
            remote(send_b.at[d, i], recv[d].at[g], b_s.at[d, i], b_r.at[d, i], (z, targets[i])).start()
        recv[d][g] = gath[d][y_of(source[0])]

    def phase_b_wait(d, source):
        for i in range(1, 8):
            slot = recv[d].at[lax.rem(g + 8 - i, 8)]
            remote(slot, slot, b_s.at[d, i], b_r.at[d, i], sibling).wait_recv()
        return recv[d][g_of(source[0])].astype(F32)

    pl.semaphore_wait(bar, NSEQ - 1 + NZ - 1)
    tail = x_ref.at[pl.ds(ROWS - HALO, HALO), :]
    phase_a(0, tail)

    def depthwise(src, base, sign, mask_ref, r0):
        m = mask_ref[r0:r0 + BLK, :]
        acc = [jnp.zeros((BLK, 128), F32) for _ in range(2)]
        for j in range(K):
            lo = base + r0 + sign * j
            inside = m >= j
            for hf in range(2):
                win = src[hf, lo:lo + BLK, :] * w_ref[j:j + 1, hf * 128:(hf + 1) * 128]
                acc[hf] = acc[hf] + jnp.where(inside, win, 0.0)
        return acc

    def forward_block(r0):
        a0, a1_ = depthwise(ext, HALO, -1, dep, r0)
        mean = jnp.sum(a0 + a1_, axis=1, keepdims=True) * (1.0 / C)
        a0, a1_ = a0 - mean, a1_ - mean
        var = jnp.sum(a0 * a0 + a1_ * a1_, axis=1, keepdims=True) * (1.0 / C)
        inv = lax.rsqrt(var + EPS)
        istd_s[r0:r0 + BLK, :] = jnp.broadcast_to(inv, (BLK, 128))
        for hf, a in enumerate((a0, a1_)):
            cols = slice(hf * 128, (hf + 1) * 128)
            n = a * inv
            normed_s[r0:r0 + BLK, cols] = n
            scaled_s[r0:r0 + BLK, cols] = (n * gain_ref[0:1, cols]).astype(BF16)

    def rows16(i):
        return pl.ds(pl.multiple_of(i * 16, 16), 16)

    def offset(k):
        return 1 + lax.rem(k + 9, NQ - 1)

    def chip(k):
        return lax.rem(xx + lax.div(k, 4), 4) * 4 + lax.rem(yy + lax.rem(k, 4), 4)

    order = [lax.rem(gz + i, CH) for i in (2, 1, 3, 0)]

    def feed_forward(o, r0, r1_):
        cols = pl.ds(pl.multiple_of(order[o] * 256, 256), 256)
        up_c = up_v[:, cols]
        down_c = down_v[cols, :]
        sc = scaled_s[r0:r1_, :]
        dy = dy_ref[r0:r1_, :]
        hid = dot(sc, up_c, 1, 0)
        gact = dot(dy, down_c, 1, 1)
        h2 = hid * hid
        th = jnp.tanh(hid * (GELU_C + (GELU_C * GELU_A) * h2))
        h1 = 0.5 + 0.5 * th
        act = hid * h1
        slope = h1 + act * (1.0 - th) * (GELU_C + (3.0 * GELU_C * GELU_A) * h2)
        act = act.astype(BF16)
        gh = (gact * slope).astype(BF16)
        out = dot(act, down_c, 1, 0)
        n = dot(gh, up_c, 1, 1)
        if o == 0:
            oacc_s[r0:r1_, :] = out
            gn_s[r0:r1_, :] = n
        else:
            oacc_s[r0:r1_, :] += out
            gn_s[r0:r1_, :] += n
        gdown = dot(act, dy, 0, 0)
        gup = dot(sc, gh, 0, 0)
        first = core == 0
        mine, theirs = jnp.where(first, gdown, gup), jnp.where(first, gup, gdown)
        if r0:
            own[o] = mine
            other[o] = theirs
        else:
            own[o] += mine
            outbound[o] = (other[o] + theirs).astype(BF16)
            remote(outbound.at[o], sib.at[o], c_s.at[o], c_r.at[o], sibling).start()

    def pair_stage(o):
        remote(sib.at[o], sib.at[o], c_s.at[o], c_r.at[o], sibling).wait_recv()
        tsum[o] = (own[o] + sib[o].astype(F32)).astype(BF16)

        def send(i):
            k = offset(i)
            qp = chip(k)
            remote(tsum.at[o, rows16(qp), :], r1.at[o, k], p_s.at[o, k], p_r.at[o, k],
                   (z, qp * 2 + core)).start()

        loop(0, NQ - 1, send)

    def norm_back(r0):
        gn = gn_s[r0:r0 + BLK, :]
        nm = normed_s[r0:r0 + BLK, :]
        prod = gn * nm
        part = jnp.sum(prod.reshape(BLK // 8, 8, C), axis=0)
        if r0 == BLK:
            gp[...] = part
        else:
            gp[...] += part
        qv = gn * gain_ref[...]
        qn = prod * gain_ref[...]
        m1 = jnp.sum(qv[:, :128] + qv[:, 128:], axis=1, keepdims=True) * (1.0 / C)
        m2 = jnp.sum(qn[:, :128] + qn[:, 128:], axis=1, keepdims=True) * (1.0 / C)
        t = qv - m1 - nm * m2
        for hf in range(2):
            gext[hf, r0:r0 + BLK, :] = t[:, hf * 128:(hf + 1) * 128] * istd_s[r0:r0 + BLK, :]

    def tap_block(r0):
        m = dep[r0:r0 + BLK, :]
        gc = [gext[hf, r0:r0 + BLK, :] for hf in range(2)]
        for j in range(K):
            lo = HALO + r0 - j
            inside = m >= j
            for hf in range(2):
                v = jnp.where(inside, gc[hf] * ext[hf, lo:lo + BLK, :], 0.0)
                part = jnp.sum(v.reshape(BLK // 8, 8, 128), axis=0)
                if r0 == BLK:
                    kp[hf, j] = part
                else:
                    kp[hf, j] += part

    def back_block(r0):
        acc = depthwise(gext, 0, 1, rem_, r0)
        for hf in range(2):
            cols = slice(hf * 128, (hf + 1) * 128)
            gin_ref[r0:r0 + BLK, cols] = (dy_ref[r0:r0 + BLK, cols].astype(F32) + acc[hf]).astype(BF16)

    later = range(BLK, ROWS, BLK)
    for r0 in later:
        forward_block(r0)
    for copy in loads[3:]:
        copy.wait()
    feed_forward(0, BLK, ROWS)
    phase_a_wait(0)
    phase_b(0, before)
    for o in range(1, CH):
        feed_forward(o, BLK, ROWS)
    for r0 in later:
        norm_back(r0)
    for r0 in later:
        tap_block(r0)

    halo = phase_b_wait(0, before)
    for hf in range(2):
        ext[hf, :HALO, :] = halo[:, hf * 128:(hf + 1) * 128]
    forward_block(0)
    for o in range(CH):
        feed_forward(o, 0, BLK)
        if o:
            pair_stage(o - 1)
    pair_stage(CH - 1)
    norm_back(0)
    for hf in range(2):
        head[:, hf * 128:(hf + 1) * 128] = gext[hf, :HALO, :].astype(BF16)
    phase_a(1, head)
    tap_block(0)
    for hf in range(2):
        taps = jnp.sum(kp[hf], axis=1)
        gain = jnp.sum(gp[:, hf * 128:(hf + 1) * 128], axis=0, keepdims=True)
        taps = jnp.concatenate([taps, gain, jnp.zeros((64 - K - 1, 128), F32)], axis=0)
        for r in range(8):
            kb[2 * r + hf] = taps[r * 8:r * 8 + 8, :]

    def send_k(i):
        p = lax.rem(q + i, NQ)
        return remote(kb.at[p], rk.at[s], k_s.at[i], k_r.at[s], (z, p * 2))

    def send_z(zp):
        return remote(zs.at[zp], r2.at[z], z_s.at[zp], z_r.at[z], (zp, s))

    def plane_sum(o):
        def got(k):
            remote(r1.at[o, k], r1.at[o, k], p_s.at[o, k], p_r.at[o, k], sibling).wait_recv()

        loop(1, NQ, got)
        acc = tsum[o, rows16(q), :].astype(F32)
        for k in range(1, NQ):
            acc = acc + r1[o, k].astype(F32)
        for j in range(4):
            rh, hf = j // 2, j % 2
            zs[order[o] * 4 + j] = acc[rh * 8:rh * 8 + 8, hf * 128:(hf + 1) * 128]
        for j in range(4):
            zp = order[o] * 4 + j

            @pl.when(zp != z)
            def _(zp=zp):
                send_z(zp).start()

    for o in range(CH):
        plane_sum(o)

    loop(1, NQ, lambda i: send_k(i).start())

    @pl.when(core == 1)
    def _():
        send_k(0).start()

    phase_a_wait(1)
    phase_b(1, after)
    out_ref[...] = (x_ref[...].astype(F32) + oacc_s[...]).astype(BF16)
    back_block(BLK)

    def got_z(i):
        zp = lax.rem(z + i, NZ)
        remote(r2.at[zp], r2.at[zp], z_s.at[zp], z_r.at[zp], sibling).wait_recv()

    loop(1, NZ, got_z)
    total = zs[z]
    for i in range(1, NZ):
        total = total + r2[lax.rem(z + i, NZ)]
    a1[z] = total * FACTOR

    def send_y(i):
        return remote(a1.at[z], a1.at[z], y_s.at[i], y_r.at[z], (lax.rem(z + i, NZ), s))

    for i in FAR_Z:
        send_y(i).start()

    @pl.when(core == 0)
    def _():
        def got(i):
            sp = lax.rem(s + i, NSEQ)
            remote(rk.at[sp], rk.at[sp], k_s.at[0], k_r.at[sp], sibling).wait_recv()

        loop(1, NSEQ, got)
        rk[s] = kb[q]
        acc = rk[0]
        for i in range(1, NSEQ):
            acc = acc + rk[i]
        rz[z] = acc
        loop(1, NZ, lambda i: remote(
            rz.at[z], rz.at[z], kz_s.at[i], kz_r.at[i], (lax.rem(z + i, NZ), s)).start())

    back_block(0)
    back_block(2 * BLK)

    def chunk_of(o):
        return lax.rem(gz + (0, 1, 3, 2)[o], CH)

    def send_q(o, k):
        piece = fin.at[core, chunk_of(o), rows16(q), :]
        return remote(piece, piece, q_s.at[o, k], q_r.at[o, k], (z, chip(k) * 2 + core))

    for o in range(CH):
        h = chunk_of(o)
        for j in range(4):
            zp = h * 4 + j

            @pl.when(zp != z)
            def _(zp=zp):
                remote(a1.at[zp], a1.at[zp], y_s.at[0], y_r.at[zp], sibling).wait_recv()

        top = jnp.concatenate([a1[4 * h], a1[4 * h + 1]], axis=1)
        bottom = jnp.concatenate([a1[4 * h + 2], a1[4 * h + 3]], axis=1)
        fin[core, h, rows16(q), :] = jnp.concatenate([top, bottom], axis=0).astype(BF16)
        loop(0, NQ - 1, lambda i, o=o: send_q(o, offset(i)).start())

    halo_g = phase_b_wait(1, after)
    for hf in range(2):
        gext[hf, ROWS:, :] = halo_g[:, hf * 128:(hf + 1) * 128]
    back_block(3 * BLK)
    stores = [
        pltpu.make_async_copy(src, dst, st_sem.at[i])
        for i, (src, dst) in enumerate((
            (out_ref, out_hbm), (gin_ref, gin_hbm), (gk_ref, gk_hbm), (gg_ref, gg_hbm)))
    ]
    stores[0].start()
    stores[1].start()

    @pl.when(core == 0)
    def _():
        def got(i):
            slot = rz.at[lax.rem(z + NZ - i, NZ)]
            remote(slot, slot, kz_s.at[i], kz_r.at[i], sibling).wait_recv()

        loop(1, NZ, got)
        acc = rz[0]
        for i in range(1, NZ):
            acc = acc + rz[i]
        kf[q] = acc * FACTOR
        loop(1, NSEQ, lambda i: remote(
            kf.at[q], kf.at[q], kf_s.at[i], kf_r.at[q], (z, lax.rem(s + i, NSEQ))).start())

    def send_f(o):
        half = fin.at[core, chunk_of(o)]
        return remote(half, half, f_s.at[o], f_r.at[o], sibling)

    def store(matrix, o):
        part = pl.ds(pl.multiple_of(chunk_of(o) * 256, 256), 256)

        @pl.when(matrix == 0)
        def _():
            pltpu.make_async_copy(fin.at[0, chunk_of(o)], gd_hbm.at[part, :], st_sem.at[4 + o]).start()

        @pl.when(matrix == 1)
        def _():
            pltpu.make_async_copy(fin.at[1, chunk_of(o)], gu_hbm.at[:, part], st_sem.at[8 + o]).start()

    for o in range(CH):
        def got_q(k, o=o):
            qs = lax.rem(xx + 4 - lax.div(k, 4), 4) * 4 + lax.rem(yy + 4 - lax.rem(k, 4), 4)
            piece = fin.at[core, chunk_of(o), rows16(qs), :]
            remote(piece, piece, q_s.at[o, k], q_r.at[o, k], sibling).wait_recv()

        loop(1, NQ, got_q)
        send_f(o).start()
        store(core, o)

    def got_kf(i):
        slot = lax.rem(q + i, NQ)
        remote(kf.at[slot], kf.at[slot], kf_s.at[0], kf_r.at[slot], sibling).wait_recv()

    loop(1, NQ, got_kf)

    @pl.when(core == 1)
    def _():
        got_kf(0)

    for hf in range(2):
        cols = slice(hf * 128, (hf + 1) * 128)
        taps = jnp.concatenate([kf[2 * r + hf] for r in range(8)], axis=0)
        gk_ref[:, cols] = taps[:K, :].astype(BF16)
        gg_ref[:, cols] = taps[K:K + 1, :]
    stores[2].start()
    stores[3].start()
    for o in range(CH):
        half = fin.at[1 - core, chunk_of(o)]
        remote(half, half, f_s.at[o], f_r.at[o], sibling).wait_recv()
        store(1 - core, o)

    for d, src in ((0, tail), (1, head)):
        for i in range(1, 4):
            remote(src, src, a_s.at[d, i], a_r.at[d, i], sibling).wait_send()
        for i in range(1, 8):
            remote(send_b.at[d, i], send_b.at[d, i], b_s.at[d, i], b_r.at[d, i], sibling).wait_send()
    for o in range(CH):
        remote(outbound.at[o], outbound.at[o], c_s.at[o], c_r.at[o], sibling).wait_send()

        def sent(k, o=o):
            slot = tsum.at[o, rows16(chip(k)), :]
            remote(slot, slot, p_s.at[o, k], p_r.at[o, k], sibling).wait_send()
            send_q(o, k).wait_send()

        loop(1, NQ, sent)
        send_f(o).wait_send()
    loop(1, NZ, lambda i: send_z(lax.rem(z + i, NZ)).wait_send())
    loop(1, NZ, lambda i: send_y(i).wait_send())
    loop(1, NQ, lambda i: send_k(i).wait_send())

    @pl.when(core == 1)
    def _():
        send_k(0).wait_send()

    @pl.when(core == 0)
    def _():
        loop(1, NZ, lambda i: remote(
            rz.at[z], rz.at[z], kz_s.at[i], kz_r.at[i], sibling).wait_send())
        loop(1, NSEQ, lambda i: remote(
            kf.at[q], kf.at[q], kf_s.at[i], kf_r.at[q], sibling).wait_send())

    for copy in stores:
        copy.wait()
    for o in range(CH):
        part = pl.ds(pl.multiple_of(chunk_of(o) * 256, 256), 256)
        pltpu.make_async_copy(fin.at[0, chunk_of(o)], gd_hbm.at[part, :], st_sem.at[4 + o]).wait()
        pltpu.make_async_copy(fin.at[1, chunk_of(o)], gu_hbm.at[:, part], st_sem.at[8 + o]).wait()


def finish(out_i, gin_i, gk_i, gu_i, gd_i, gg_i, out_o, gin_o, gk_o, gu_o, gd_o, gg_o, sem):
    pairs = ((out_i, out_o), (gin_i, gin_o), (gk_i, gk_o), (gu_i, gu_o), (gd_i, gd_o))
    copies = [pltpu.make_async_copy(a, b, sem.at[i]) for i, (a, b) in enumerate(pairs)]
    for copy in copies:
        copy.start()
    gg_o[...] = gg_i[0, :].astype(BF16)
    for copy in copies:
        copy.wait()


def per_device(inputs, cotangent, lengths, placed, conv_weight, norm_gain, up_weight, down_weight):
    vm = pl.BlockSpec(memory_space=pltpu.VMEM)
    sm = pl.BlockSpec(memory_space=pltpu.SMEM)
    hb = pl.BlockSpec(memory_space=pltpu.HBM)
    V, D = pltpu.VMEM, pltpu.SemaphoreType.DMA
    out, gin, gk, gg, gu, gd = pl.pallas_call(
        kernel,
        out_shape=(
            jax.ShapeDtypeStruct((ROWS, C), BF16),
            jax.ShapeDtypeStruct((ROWS, C), BF16),
            jax.ShapeDtypeStruct((K, C), BF16),
            jax.ShapeDtypeStruct((1, C), F32),
            jax.ShapeDtypeStruct((C, HID), BF16),
            jax.ShapeDtypeStruct((HID, C), BF16),
        ),
        in_specs=[sm, sm, hb, hb, hb, hb, hb, hb],
        out_specs=(hb,) * 6,
        scratch_shapes=[
            V((ROWS, C), BF16), V((ROWS, C), BF16), V((K, C), BF16), V((1, C), F32),
            V((2, CH, 256, 256), BF16),
            V((ROWS, C), BF16), V((ROWS, C), BF16), V((K, C), F32), V((1, C), F32),
            V((C, HID), BF16), V((HID, C), BF16),
            V((4, HALO, C), BF16), V((4, HALO, C), BF16), V((2, 8, HALO, C), BF16),
            V((8, HALO, C), BF16), V((8, HALO, C), BF16),
            V((HALO, C), BF16),
            V((2, HALO + ROWS, 128), F32), V((2, ROWS + HALO, 128), F32),
            V((ROWS, 128), jnp.int32), V((ROWS, 128), jnp.int32),
            V((ROWS, C), F32), V((ROWS, 128), F32), V((ROWS, C), BF16),
            V((ROWS, C), F32), V((ROWS, C), F32),
            V((CH, 256, 256), F32), V((CH, 256, 256), F32),
            V((CH, 256, 256), BF16), V((CH, 256, 256), BF16), V((CH, 256, 256), BF16),
            V((CH, NQ, 16, 256), BF16),
            V((NZ, 8, 128), F32), V((NZ, 8, 128), F32), V((NZ, 8, 128), F32),
            V((2, K, 8, 128), F32), V((8, C), F32), V((NQ, 8, 128), F32), V((NSEQ, 8, 128), F32),
            V((NZ, 8, 128), F32), V((NQ, 8, 128), F32),
            D((6,)), D((2, 4)), D((2, 4)), D((2, 8)), D((2, 8)), D((CH,)), D((CH,)),
            D((CH, NQ)), D((CH, NQ)), D((NZ,)), D((NZ,)), D((NZ,)), D((NZ,)), D((CH, NQ)), D((CH, NQ)),
            D((CH,)), D((CH,)), D((NQ,)), D((NSEQ,)), D((NZ,)), D((NZ,)), D((NSEQ,)), D((NQ,)), D((12,)),
        ],
        compiler_params=pltpu.CompilerParams(
            collective_id=0, has_side_effects=True, vmem_limit_bytes=VM_BYTES
        ),
    )(
        lengths, placed, inputs.reshape(ROWS, C), cotangent.reshape(ROWS, C), conv_weight,
        norm_gain.reshape(1, C), up_weight, down_weight,
    )
    out, gin, gk, gu, gd, gg = pl.pallas_call(
        finish,
        out_shape=(
            jax.ShapeDtypeStruct((ROWS, C), BF16),
            jax.ShapeDtypeStruct((ROWS, C), BF16),
            jax.ShapeDtypeStruct((K, C), BF16),
            jax.ShapeDtypeStruct((C, HID), BF16),
            jax.ShapeDtypeStruct((HID, C), BF16),
            jax.ShapeDtypeStruct((C,), BF16),
        ),
        in_specs=[hb, hb, hb, hb, hb, vm],
        out_specs=(hb, hb, hb, hb, hb, vm),
        scratch_shapes=[D((5,))],
    )(out, gin, gk, gu, gd, gg)
    return (
        out.reshape(inputs.shape), gin.reshape(inputs.shape), gk, gg, gu, gd,
    )


def solution(mesh):
    tok = P("dp", "seq", None, None)
    return jax.shard_map(
        per_device,
        mesh=mesh,
        in_specs=(tok, tok, P("dp", None), P("dp", None), P(), P(), P(), P()),
        out_specs=(tok, tok, P(), P(), P(), P()),
        check_vma=False,
    )
```

time: 81.7 us -> 106 us (1.30)
  Pallas kernels: 71.3 us -> 105 us
  local copies, waits for them, and re-layouts: 8.89 us -> 0 us
    pallas_call x0 -> x1, Pallas kernels: none -> 42.9 us  [per_device(): pl.pallas_call(finish, out_shape=(jax.ShapeDtypeStruct((ROWS, C), BF16),...]
    pallas_call x1, Pallas kernels: 71.3 us -> 62.3 us  [per_device(): pl.pallas_call(kernel, out_shape=(jax.ShapeDtypeStruct((ROWS, C), BF16),...]
    unnamed x21 -> x0, local copies, waits for them, and re-layouts: 8.89 us -> none
where the time goes in v2:
time: 106 us
  Pallas kernels  105 us (99%)
    pallas_call x1, Pallas kernels, per_device(): pl.pallas_call(kernel, out_shape=(jax.ShapeDtypeStruct((ROWS, C), BF16),...  62.3 us
    pallas_call x1, Pallas kernels, per_device(): pl.pallas_call(finish, out_shape=(jax.ShapeDtypeStruct((ROWS, C), BF16),...  42.9 us

profile of v2, /device:TPU:1, one launch (start us, length us, event | category | flops | bytes accessed | tf_op | source)
XLA Modules:
  0.0 105.8 jit_solution(11554657042665937898)
XLA Ops:
  0.6 62.3 %shard_map.127 = (bf16[256,256]{1,0:T(8,128)(2,1)}, bf16[256,256]{1,0:T(8,128)(2,1)}, bf16[51,256]{1,0:T(8,128)(2,1)}, f32[1,256]{1,0:T(1,128)}, bf16[256,1024]{1,0:T(8,128)(2,1)}, /*index=5*/bf16[1024,256]{1,0:T(8,128)(2,1)}) custom-call(s32[1,8]{1,0:T(1,128)} %lengths.1, s32[1,32]{1,0:T(1,128)} %placed.1, bf16[256,256]{1,0:T(8,128)(2,1)} %bitcast.5, ...), custom_call_target="tpu_custom_call" | custom-call | tf_op jit(solution)/shard_map/pallas_call | solution.py:526
  62.9 42.9 %shard_map.128 = (bf16[256,256]{1,0:T(8,128)(2,1)}, bf16[256,256]{1,0:T(8,128)(2,1)}, bf16[51,256]{1,0:T(8,128)(2,1)}, bf16[256,1024]{1,0:T(8,128)(2,1)}, bf16[1...) custom-call(bf16[256,256]{1,0:T(8,128)(2,1)} %get-tuple-element.18.out_i, bf16[256,256]{1,0:T(8,128)(2,1)} %get-tuple-element.19.gin_i, ...), custom_call_target="tpu_custom_call" | custom-call | tf_op jit(solution)/shard_map/pallas_call | solution.py:567

commit v3 on v2

--- a/solution.py
+++ b/solution.py
@@ -508,13 +508,18 @@
         pltpu.make_async_copy(fin.at[1, chunk_of(o)], gu_hbm.at[:, part], st_sem.at[8 + o]).wait()
 
 
-def finish(out_i, gin_i, gk_i, gu_i, gd_i, gg_i, out_o, gin_o, gk_o, gu_o, gd_o, gg_o, sem):
-    pairs = ((out_i, out_o), (gin_i, gin_o), (gk_i, gk_o), (gu_i, gu_o), (gd_i, gd_o))
-    copies = [pltpu.make_async_copy(a, b, sem.at[i]) for i, (a, b) in enumerate(pairs)]
-    for copy in copies:
+def finish(*refs):
+    ins, outs, held = refs[:5], refs[6:11], refs[12:17]
+    gg_i, gg_o, get, put = refs[5], refs[11], refs[17], refs[18]
+    loads = [pltpu.make_async_copy(a, b, get.at[i]) for i, (a, b) in enumerate(zip(ins, held))]
+    stores = [pltpu.make_async_copy(a, b, put.at[i]) for i, (a, b) in enumerate(zip(held, outs))]
+    for copy in loads:
         copy.start()
     gg_o[...] = gg_i[0, :].astype(BF16)
-    for copy in copies:
+    for load, store in zip(loads, stores):
+        load.wait()
+        store.start()
+    for copy in stores:
         copy.wait()
 
 
@@ -576,7 +581,10 @@
         ),
         in_specs=[hb, hb, hb, hb, hb, vm],
         out_specs=(hb, hb, hb, hb, hb, vm),
-        scratch_shapes=[D((5,))],
+        scratch_shapes=[
+            V((ROWS, C), BF16), V((ROWS, C), BF16), V((K, C), BF16), V((C, HID), BF16), V((HID, C), BF16),
+            D((5,)), D((5,)),
+        ],
     )(out, gin, gk, gu, gd, gg)
     return (
         out.reshape(inputs.shape), gin.reshape(inputs.shape), gk, gg, gu, gd,

time: 106 us -> 66.5 us (0.63)
  Pallas kernels: 105 us -> 65.7 us
    pallas_call x1, Pallas kernels: 42.9 us -> 3.43 us  [per_device(): pl.pallas_call(finish, out_shape=(jax.ShapeDtypeStruct((ROWS, C), BF16),...]
where the time goes in v3:
time: 66.5 us; the launch traced here: 66.4 us
  Pallas kernels  65.7 us (99%)
    pallas_call x1, Pallas kernels, per_device(): pl.pallas_call(kernel, out_shape=(jax.ShapeDtypeStruct((ROWS, C), BF16),...  62.3 us
    pallas_call x1, Pallas kernels, per_device(): pl.pallas_call(finish, out_shape=(jax.ShapeDtypeStruct((ROWS, C), BF16),...  3.43 us

profile of v3, /device:TPU:1, one launch (start us, length us, event | category | flops | bytes accessed | tf_op | source)
XLA Modules:
  0.0 66.4 jit_solution(6251703958253843964)
XLA Ops:
  0.6 62.3 %shard_map.127 = (bf16[256,256]{1,0:T(8,128)(2,1)}, bf16[256,256]{1,0:T(8,128)(2,1)}, bf16[51,256]{1,0:T(8,128)(2,1)}, f32[1,256]{1,0:T(1,128)}, bf16[256,1024]{1,0:T(8,128)(2,1)}, /*index=5*/bf16[1024,256]{1,0:T(8,128)(2,1)}) custom-call(s32[1,8]{1,0:T(1,128)} %lengths.1, s32[1,32]{1,0:T(1,128)} %placed.1, bf16[256,256]{1,0:T(8,128)(2,1)} %bitcast.5, ...), custom_call_target="tpu_custom_call" | custom-call | tf_op jit(solution)/shard_map/pallas_call | solution.py:531
  62.9 3.4 %shard_map.128 = (bf16[256,256]{1,0:T(8,128)(2,1)}, bf16[256,256]{1,0:T(8,128)(2,1)}, bf16[51,256]{1,0:T(8,128)(2,1)}, bf16[256,1024]{1,0:T(8,128)(2,1)}, bf16[1...) custom-call(bf16[256,256]{1,0:T(8,128)(2,1)} %get-tuple-element.18.refs_0_, bf16[256,256]{1,0:T(8,128)(2,1)} %get-tuple-element.19.refs_1_, ...), custom_call_target="tpu_custom_call" | custom-call | tf_op jit(solution)/shard_map/pallas_call | solution.py:572

commit v4 on v2

--- a/solution.py
+++ b/solution.py
@@ -20,11 +20,12 @@
 HALO = 64
 BLK = 64
 NZ, NSEQ, NQ = 16, 32, 16
-VM_BYTES = 60 * 2**20
+VM_BYTES = 40 * 2**20
 CH = 4
 FACTOR = 1.0 / math.sqrt(NZ * NSEQ * ROWS)
 GELU_C = math.sqrt(2.0 / math.pi)
 GELU_A = 0.044715
+FAR_Q = (10, 11, 14, 9, 6, 15, 13, 7, 5, 8, 2, 12, 3, 4, 1)
 FAR_Z = (8, 7, 9, 6, 10, 5, 11, 4, 12, 3, 13, 2, 14, 1, 15)
 
 
@@ -47,13 +48,13 @@
 
 
 def kernel(
-    lengths, placed, x_hbm, dy_hbm, w_hbm, gain_hbm, up_hbm, down_hbm,
-    out_hbm, gin_hbm, gk_hbm, gg_hbm, gu_hbm, gd_hbm,
-    out_ref, gin_ref, gk_ref, gg_ref, fin, x_ref, dy_ref, w_ref, gain_ref, up_v, down_v,
+    lengths_hbm, placed_hbm, x_hbm, dy_hbm, w_hbm, gain_hbm, up_hbm, down_hbm,
+    out_ref, gin_ref, gk_ref, gg_ref, fin,
+    lengths, placed, x_ref, dy_ref, w_ref, gain_ref, up_v, down_v,
     gath0, gath1, send_b, recv0, recv1, head, ext, gext, dep, rem_, normed_s, istd_s, scaled_s,
     gn_s, oacc_s, own, other, outbound, sib, tsum, r1, zs, r2, a1, kp, gp, kb, rk, rz, kf,
     ld_sem, a_s, a_r, b_s, b_r, c_s, c_r, p_s, p_r, z_s, z_r, y_s, y_r, q_s, q_r, f_s, f_r,
-    k_s, k_r, kz_s, kz_r, kf_s, kf_r, st_sem,
+    k_s, k_r, kz_s, kz_r, kf_s, kf_r,
 ):
     z = lax.axis_index("dp")
     s = lax.axis_index("seq")
@@ -66,19 +67,22 @@
     sibling = (z, q * 2 + 1 - core)
     gath, recv = (gath0, gath1), (recv0, recv1)
 
+    loads = [
+        pltpu.make_async_copy(src, dst, ld_sem.at[i])
+        for i, (src, dst) in enumerate((
+            (placed_hbm, placed), (lengths_hbm, lengths), (x_hbm, x_ref), (w_hbm, w_ref), (gain_hbm, gain_ref),
+            (dy_hbm, dy_ref), (up_hbm, up_v), (down_hbm, down_v)))
+    ]
+    for copy in loads:
+        copy.start()
+
     bar = pltpu.get_barrier_semaphore()
     for i in FAR_Z:
         pl.semaphore_signal(bar, inc=1, device_id=(lax.rem(z + i, NZ), s), device_id_type=MESH)
     loop(0, NSEQ - 1, lambda i: pl.semaphore_signal(
         bar, inc=1, device_id=(z, lax.rem(s + 1 + lax.rem(i + 19, NSEQ - 1), NSEQ)), device_id_type=MESH))
-    loads = [
-        pltpu.make_async_copy(src, dst, ld_sem.at[i])
-        for i, (src, dst) in enumerate((
-            (x_hbm, x_ref), (w_hbm, w_ref), (gain_hbm, gain_ref),
-            (dy_hbm, dy_ref), (up_hbm, up_v), (down_hbm, down_v)))
-    ]
-    for copy in loads:
-        copy.start()
+    loads[0].wait()
+    loads[1].wait()
 
     def target(i):
         gt = lax.rem(g + i, 8)
@@ -115,11 +119,11 @@
     for e in reversed(ends):
         stop = jnp.where(e > pos, e, stop)
     rem_[...] = stop - 1 - pos
-    loads[0].wait()
+    loads[2].wait()
     for hf in range(2):
         ext[hf, HALO:, :] = x_ref[:, hf * 128:(hf + 1) * 128].astype(F32)
-    loads[1].wait()
-    loads[2].wait()
+    loads[3].wait()
+    loads[4].wait()
 
     def phase_a(d, src):
         for i in range(1, 4):
@@ -175,11 +179,14 @@
     def rows16(i):
         return pl.ds(pl.multiple_of(i * 16, 16), 16)
 
-    def offset(k):
-        return 1 + lax.rem(k + 9, NQ - 1)
+    x_to = [lax.rem(xx + i, 4) for i in range(4)]
+    y_to = [lax.rem(yy + i, 4) for i in range(4)]
 
     def chip(k):
-        return lax.rem(xx + lax.div(k, 4), 4) * 4 + lax.rem(yy + lax.rem(k, 4), 4)
+        return x_to[k // 4] * 4 + y_to[k % 4]
+
+    def chip_back(k):
+        return x_to[-(k // 4) % 4] * 4 + y_to[-(k % 4) % 4]
 
     order = [lax.rem(gz + i, CH) for i in (2, 1, 3, 0)]
 
@@ -218,17 +225,17 @@
             outbound[o] = (other[o] + theirs).astype(BF16)
             remote(outbound.at[o], sib.at[o], c_s.at[o], c_r.at[o], sibling).start()
 
+    def send_p(u, k):
+        qp = chip(k)
+        return remote(tsum.at[pl.ds(2 * u, 2), rows16(qp), :], r1.at[u, k], p_s.at[u, k], p_r.at[u],
+                      (z, qp * 2 + core))
+
     def pair_stage(o):
         remote(sib.at[o], sib.at[o], c_s.at[o], c_r.at[o], sibling).wait_recv()
         tsum[o] = (own[o] + sib[o].astype(F32)).astype(BF16)
-
-        def send(i):
-            k = offset(i)
-            qp = chip(k)
-            remote(tsum.at[o, rows16(qp), :], r1.at[o, k], p_s.at[o, k], p_r.at[o, k],
-                   (z, qp * 2 + core)).start()
-
-        loop(0, NQ - 1, send)
+        if o % 2:
+            for k in FAR_Q:
+                send_p(o // 2, k).start()
 
     def norm_back(r0):
         gn = gn_s[r0:r0 + BLK, :]
@@ -270,7 +277,7 @@
     later = range(BLK, ROWS, BLK)
     for r0 in later:
         forward_block(r0)
-    for copy in loads[3:]:
+    for copy in loads[5:]:
         copy.wait()
     feed_forward(0, BLK, ROWS)
     phase_a_wait(0)
@@ -303,35 +310,35 @@
         for r in range(8):
             kb[2 * r + hf] = taps[r * 8:r * 8 + 8, :]
 
-    def send_k(i):
-        p = lax.rem(q + i, NQ)
-        return remote(kb.at[p], rk.at[s], k_s.at[i], k_r.at[s], (z, p * 2))
+    def send_k(k):
+        p = chip(k) * 2
+        slot = lax.rem(p - s + NSEQ, NSEQ)
+        return remote(kb.at[chip(k)], rk.at[slot], k_s.at[k], k_r.at[0], (z, p))
 
     def send_z(zp):
-        return remote(zs.at[zp], r2.at[z], z_s.at[zp], z_r.at[z], (zp, s))
-
-    def plane_sum(o):
-        def got(k):
-            remote(r1.at[o, k], r1.at[o, k], p_s.at[o, k], p_r.at[o, k], sibling).wait_recv()
-
-        loop(1, NQ, got)
-        acc = tsum[o, rows16(q), :].astype(F32)
-        for k in range(1, NQ):
-            acc = acc + r1[o, k].astype(F32)
-        for j in range(4):
-            rh, hf = j // 2, j % 2
-            zs[order[o] * 4 + j] = acc[rh * 8:rh * 8 + 8, hf * 128:(hf + 1) * 128]
-        for j in range(4):
-            zp = order[o] * 4 + j
-
-            @pl.when(zp != z)
-            def _(zp=zp):
-                send_z(zp).start()
-
-    for o in range(CH):
-        plane_sum(o)
-
-    loop(1, NQ, lambda i: send_k(i).start())
+        i = lax.rem(zp - z + NZ, NZ)
+        return remote(zs.at[zp], r2.at[i], z_s.at[i], z_r.at[0], (zp, s))
+
+    for u in range(CH // 2):
+        got = r1.at[u, pl.ds(1, NQ - 1)]
+        remote(got, got, p_s.at[u, 0], p_r.at[u], sibling).wait_recv()
+        for v in range(2):
+            o = 2 * u + v
+            acc = tsum[o, rows16(q), :].astype(F32)
+            for k in range(1, NQ):
+                acc = acc + r1[u, k, v].astype(F32)
+            for j in range(4):
+                rh, hf = j // 2, j % 2
+                zs[order[o] * 4 + j] = acc[rh * 8:rh * 8 + 8, hf * 128:(hf + 1) * 128]
+            for j in range(4):
+                zp = order[o] * 4 + j
+
+                @pl.when(zp != z)
+                def _(zp=zp):
+                    send_z(zp).start()
+
+    for k in range(1, NQ):
+        send_k(k).start()
 
     @pl.when(core == 1)
     def _():
@@ -342,14 +349,11 @@
     out_ref[...] = (x_ref[...].astype(F32) + oacc_s[...]).astype(BF16)
     back_block(BLK)
 
-    def got_z(i):
-        zp = lax.rem(z + i, NZ)
-        remote(r2.at[zp], r2.at[zp], z_s.at[zp], z_r.at[zp], sibling).wait_recv()
-
-    loop(1, NZ, got_z)
+    got = r2.at[pl.ds(1, NZ - 1)]
+    remote(got, got, z_s.at[0], z_r.at[0], sibling).wait_recv()
     total = zs[z]
     for i in range(1, NZ):
-        total = total + r2[lax.rem(z + i, NZ)]
+        total = total + r2[i]
     a1[z] = total * FACTOR
 
     def send_y(i):
@@ -360,13 +364,9 @@
 
     @pl.when(core == 0)
     def _():
-        def got(i):
-            sp = lax.rem(s + i, NSEQ)
-            remote(rk.at[sp], rk.at[sp], k_s.at[0], k_r.at[sp], sibling).wait_recv()
-
-        loop(1, NSEQ, got)
-        rk[s] = kb[q]
-        acc = rk[0]
+        got = rk.at[pl.ds(1, NSEQ - 1)]
+        remote(got, got, k_s.at[0], k_r.at[0], sibling).wait_recv()
+        acc = kb[q]
         for i in range(1, NSEQ):
             acc = acc + rk[i]
         rz[z] = acc
@@ -395,19 +395,13 @@
         top = jnp.concatenate([a1[4 * h], a1[4 * h + 1]], axis=1)
         bottom = jnp.concatenate([a1[4 * h + 2], a1[4 * h + 3]], axis=1)
         fin[core, h, rows16(q), :] = jnp.concatenate([top, bottom], axis=0).astype(BF16)
-        loop(0, NQ - 1, lambda i, o=o: send_q(o, offset(i)).start())
+        for k in FAR_Q:
+            send_q(o, k).start()
 
     halo_g = phase_b_wait(1, after)
     for hf in range(2):
         gext[hf, ROWS:, :] = halo_g[:, hf * 128:(hf + 1) * 128]
     back_block(3 * BLK)
-    stores = [
-        pltpu.make_async_copy(src, dst, st_sem.at[i])
-        for i, (src, dst) in enumerate((
-            (out_ref, out_hbm), (gin_ref, gin_hbm), (gk_ref, gk_hbm), (gg_ref, gg_hbm)))
-    ]
-    stores[0].start()
-    stores[1].start()
 
     @pl.when(core == 0)
     def _():
@@ -427,49 +421,6 @@
         half = fin.at[core, chunk_of(o)]
         return remote(half, half, f_s.at[o], f_r.at[o], sibling)
 
-    def store(matrix, o):
-        part = pl.ds(pl.multiple_of(chunk_of(o) * 256, 256), 256)
-
-        @pl.when(matrix == 0)
-        def _():
-            pltpu.make_async_copy(fin.at[0, chunk_of(o)], gd_hbm.at[part, :], st_sem.at[4 + o]).start()
-
-        @pl.when(matrix == 1)
-        def _():
-            pltpu.make_async_copy(fin.at[1, chunk_of(o)], gu_hbm.at[:, part], st_sem.at[8 + o]).start()
-
-    for o in range(CH):
-        def got_q(k, o=o):
-            qs = lax.rem(xx + 4 - lax.div(k, 4), 4) * 4 + lax.rem(yy + 4 - lax.rem(k, 4), 4)
-            piece = fin.at[core, chunk_of(o), rows16(qs), :]
-            remote(piece, piece, q_s.at[o, k], q_r.at[o, k], sibling).wait_recv()
-
-        loop(1, NQ, got_q)
-        send_f(o).start()
-        store(core, o)
-
-    def got_kf(i):
-        slot = lax.rem(q + i, NQ)
-        remote(kf.at[slot], kf.at[slot], kf_s.at[0], kf_r.at[slot], sibling).wait_recv()
-
-    loop(1, NQ, got_kf)
-
-    @pl.when(core == 1)
-    def _():
-        got_kf(0)
-
-    for hf in range(2):
-        cols = slice(hf * 128, (hf + 1) * 128)
-        taps = jnp.concatenate([kf[2 * r + hf] for r in range(8)], axis=0)
-        gk_ref[:, cols] = taps[:K, :].astype(BF16)
-        gg_ref[:, cols] = taps[K:K + 1, :]
-    stores[2].start()
-    stores[3].start()
-    for o in range(CH):
-        half = fin.at[1 - core, chunk_of(o)]
-        remote(half, half, f_s.at[o], f_r.at[o], sibling).wait_recv()
-        store(1 - core, o)
-
     for d, src in ((0, tail), (1, head)):
         for i in range(1, 4):
             remote(src, src, a_s.at[d, i], a_r.at[d, i], sibling).wait_send()
@@ -477,17 +428,43 @@
             remote(send_b.at[d, i], send_b.at[d, i], b_s.at[d, i], b_r.at[d, i], sibling).wait_send()
     for o in range(CH):
         remote(outbound.at[o], outbound.at[o], c_s.at[o], c_r.at[o], sibling).wait_send()
-
-        def sent(k, o=o):
-            slot = tsum.at[o, rows16(chip(k)), :]
-            remote(slot, slot, p_s.at[o, k], p_r.at[o, k], sibling).wait_send()
+    for k in range(1, NQ):
+        for u in range(CH // 2):
+            send_p(u, k).wait_send()
+        send_k(k).wait_send()
+    for i in range(1, NZ):
+        remote(zs.at[0], r2.at[i], z_s.at[i], z_r.at[0], sibling).wait_send()
+        send_y(i).wait_send()
+
+    for o in range(CH):
+        for k in FAR_Q[::-1]:
+            piece = fin.at[core, chunk_of(o), rows16(chip_back(k)), :]
+            remote(piece, piece, q_s.at[o, k], q_r.at[o, k], sibling).wait_recv()
+        send_f(o).start()
+
+    def got_kf(i):
+        slot = lax.rem(q + i, NQ)
+        remote(kf.at[slot], kf.at[slot], kf_s.at[0], kf_r.at[slot], sibling).wait_recv()
+
+    loop(1, NQ, got_kf)
+
+    @pl.when(core == 1)
+    def _():
+        got_kf(0)
+
+    for hf in range(2):
+        cols = slice(hf * 128, (hf + 1) * 128)
+        taps = jnp.concatenate([kf[2 * r + hf] for r in range(8)], axis=0)
+        gk_ref[:, cols] = taps[:K, :].astype(BF16)
+        gg_ref[:, cols] = taps[K:K + 1, :]
+    for o in range(CH):
+        half = fin.at[1 - core, chunk_of(o)]
+        remote(half, half, f_s.at[o], f_r.at[o], sibling).wait_recv()
+
+    for o in range(CH):
+        for k in range(1, NQ):
             send_q(o, k).wait_send()
-
-        loop(1, NQ, sent)
         send_f(o).wait_send()
-    loop(1, NZ, lambda i: send_z(lax.rem(z + i, NZ)).wait_send())
-    loop(1, NZ, lambda i: send_y(i).wait_send())
-    loop(1, NQ, lambda i: send_k(i).wait_send())
 
     @pl.when(core == 1)
     def _():
@@ -500,16 +477,12 @@
         loop(1, NSEQ, lambda i: remote(
             kf.at[q], kf.at[q], kf_s.at[i], kf_r.at[q], sibling).wait_send())
 
-    for copy in stores:
-        copy.wait()
-    for o in range(CH):
-        part = pl.ds(pl.multiple_of(chunk_of(o) * 256, 256), 256)
-        pltpu.make_async_copy(fin.at[0, chunk_of(o)], gd_hbm.at[part, :], st_sem.at[4 + o]).wait()
-        pltpu.make_async_copy(fin.at[1, chunk_of(o)], gu_hbm.at[:, part], st_sem.at[8 + o]).wait()
-
-
-def finish(out_i, gin_i, gk_i, gu_i, gd_i, gg_i, out_o, gin_o, gk_o, gu_o, gd_o, gg_o, sem):
-    pairs = ((out_i, out_o), (gin_i, gin_o), (gk_i, gk_o), (gu_i, gu_o), (gd_i, gd_o))
+
+def finish(out_i, gin_i, gk_i, gg_i, fin, out_o, gin_o, gk_o, gu_o, gd_o, gg_o, sem):
+    pairs = [(out_i, out_o), (gin_i, gin_o), (gk_i, gk_o)]
+    for h in range(CH):
+        part = pl.ds(h * 256, 256)
+        pairs += [(fin.at[0, h], gd_o.at[part, :]), (fin.at[1, h], gu_o.at[:, part])]
     copies = [pltpu.make_async_copy(a, b, sem.at[i]) for i, (a, b) in enumerate(pairs)]
     for copy in copies:
         copy.start()
@@ -520,24 +493,17 @@
 
 def per_device(inputs, cotangent, lengths, placed, conv_weight, norm_gain, up_weight, down_weight):
     vm = pl.BlockSpec(memory_space=pltpu.VMEM)
-    sm = pl.BlockSpec(memory_space=pltpu.SMEM)
     hb = pl.BlockSpec(memory_space=pltpu.HBM)
     V, D = pltpu.VMEM, pltpu.SemaphoreType.DMA
-    out, gin, gk, gg, gu, gd = pl.pallas_call(
+    held = pl.pallas_call(
         kernel,
         out_shape=(
-            jax.ShapeDtypeStruct((ROWS, C), BF16),
-            jax.ShapeDtypeStruct((ROWS, C), BF16),
-            jax.ShapeDtypeStruct((K, C), BF16),
-            jax.ShapeDtypeStruct((1, C), F32),
-            jax.ShapeDtypeStruct((C, HID), BF16),
-            jax.ShapeDtypeStruct((HID, C), BF16),
+            V((ROWS, C), BF16), V((ROWS, C), BF16), V((K, C), BF16), V((1, C), F32), V((2, CH, 256, 256), BF16),
         ),
-        in_specs=[sm, sm, hb, hb, hb, hb, hb, hb],
-        out_specs=(hb,) * 6,
+        in_specs=[hb] * 8,
+        out_specs=(vm,) * 5,
         scratch_shapes=[
-            V((ROWS, C), BF16), V((ROWS, C), BF16), V((K, C), BF16), V((1, C), F32),
-            V((2, CH, 256, 256), BF16),
+            pltpu.SMEM((1, TRACES), jnp.int32), pltpu.SMEM((1, NSEQ), jnp.int32),
             V((ROWS, C), BF16), V((ROWS, C), BF16), V((K, C), F32), V((1, C), F32),
             V((C, HID), BF16), V((HID, C), BF16),
             V((4, HALO, C), BF16), V((4, HALO, C), BF16), V((2, 8, HALO, C), BF16),
@@ -549,20 +515,21 @@
             V((ROWS, C), F32), V((ROWS, C), F32),
             V((CH, 256, 256), F32), V((CH, 256, 256), F32),
             V((CH, 256, 256), BF16), V((CH, 256, 256), BF16), V((CH, 256, 256), BF16),
-            V((CH, NQ, 16, 256), BF16),
+            V((CH // 2, NQ, 2, 16, 256), BF16),
             V((NZ, 8, 128), F32), V((NZ, 8, 128), F32), V((NZ, 8, 128), F32),
             V((2, K, 8, 128), F32), V((8, C), F32), V((NQ, 8, 128), F32), V((NSEQ, 8, 128), F32),
             V((NZ, 8, 128), F32), V((NQ, 8, 128), F32),
-            D((6,)), D((2, 4)), D((2, 4)), D((2, 8)), D((2, 8)), D((CH,)), D((CH,)),
-            D((CH, NQ)), D((CH, NQ)), D((NZ,)), D((NZ,)), D((NZ,)), D((NZ,)), D((CH, NQ)), D((CH, NQ)),
-            D((CH,)), D((CH,)), D((NQ,)), D((NSEQ,)), D((NZ,)), D((NZ,)), D((NSEQ,)), D((NQ,)), D((12,)),
+            D((8,)), D((2, 4)), D((2, 4)), D((2, 8)), D((2, 8)), D((CH,)), D((CH,)),
+            D((CH // 2, NQ)), D((CH // 2,)), D((NZ,)), D((1,)), D((NZ,)), D((NZ,)), D((CH, NQ)), D((CH, NQ)),
+            D((CH,)), D((CH,)), D((NQ,)), D((1,)), D((NZ,)), D((NZ,)), D((NSEQ,)), D((NQ,)),
         ],
         compiler_params=pltpu.CompilerParams(
             collective_id=0, has_side_effects=True, vmem_limit_bytes=VM_BYTES
         ),
     )(
-        lengths, placed, inputs.reshape(ROWS, C), cotangent.reshape(ROWS, C), conv_weight,
-        norm_gain.reshape(1, C), up_weight, down_weight,
+        *(pltpu.with_memory_space_constraint(a, pltpu.HBM) for a in (
+            lengths, placed, inputs.reshape(ROWS, C), cotangent.reshape(ROWS, C), conv_weight,
+            norm_gain.reshape(1, C), up_weight, down_weight)),
     )
     out, gin, gk, gu, gd, gg = pl.pallas_call(
         finish,
@@ -574,10 +541,11 @@
             jax.ShapeDtypeStruct((HID, C), BF16),
             jax.ShapeDtypeStruct((C,), BF16),
         ),
-        in_specs=[hb, hb, hb, hb, hb, vm],
+        in_specs=[vm] * 5,
         out_specs=(hb, hb, hb, hb, hb, vm),
-        scratch_shapes=[D((5,))],
-    )(out, gin, gk, gu, gd, gg)
+        scratch_shapes=[D((3 + 2 * CH,))],
+        compiler_params=pltpu.CompilerParams(vmem_limit_bytes=2**20),
+    )(*held)
     return (
         out.reshape(inputs.shape), gin.reshape(inputs.shape), gk, gg, gu, gd,
     )

time: 106 us -> 63.4 us (0.60)
  Pallas kernels: 105 us -> 62.7 us
    pallas_call x1, Pallas kernels: 42.9 us -> 1.66 us  [per_device(): pl.pallas_call(finish, out_shape=(jax.ShapeDtypeStruct((ROWS, C), BF16),...]
    pallas_call x1, Pallas kernels: 62.3 us -> 61 us  [per_device(): pl.pallas_call(kernel, out_shape=(V((ROWS, C), BF16), V((ROWS, C), BF16),...]
where the time goes in v4:
time: 63.4 us; the launch traced here: 63.3 us
  Pallas kernels  62.7 us (99%)
  between operations  0.64 us (1%)
    pallas_call x1, Pallas kernels, per_device(): pl.pallas_call(kernel, out_shape=(V((ROWS, C), BF16), V((ROWS, C), BF16),...  61 us
    pallas_call x1, Pallas kernels, per_device(): pl.pallas_call(finish, out_shape=(jax.ShapeDtypeStruct((ROWS, C), BF16),...  1.66 us

profile of v4, /device:TPU:1, one launch (start us, length us, event | category | flops | bytes accessed | tf_op | source)
XLA Modules:
  0.0 63.3 jit_solution(1906755744911913126)
XLA Ops:
  0.6 61.0 %shard_map.127 = (bf16[256,256]{1,0:T(8,128)(2,1)S(1)}, bf16[256,256]{1,0:T(8,128)(2,1)S(1)}, bf16[51,256]{1,0:T(8,128)(2,1)S(1)}, f32[1,256]{1,0:T(1,128)S(1)}, bf16[2,4,256,256]{3,2,1,0:T(8,128)(2,1)S(1)}) custom-call(s32[1,8]{1,0:T(1,128)} %lengths_hbm.1, s32[1,32]{1,0:T(1,128)} %placed_hbm.1, bf16[256,256]{1,0:T(8,128)(2,1)} %bitcast.5, ...), custom_call_target="tpu_custom_call" | custom-call | tf_op jit(solution)/shard_map/pallas_call | solution.py:498
  61.6 1.7 %shard_map.128 = (bf16[256,256]{1,0:T(8,128)(2,1)}, bf16[256,256]{1,0:T(8,128)(2,1)}, bf16[51,256]{1,0:T(8,128)(2,1)}, bf16[256,1024]{1,0:T(8,128)(2,1)}, bf16[1...) custom-call(bf16[256,256]{1,0:T(8,128)(2,1)S(1)} %get-tuple-element.17.out_i, bf16[256,256]{1,0:T(8,128)(2,1)S(1)} %get-tuple-element.18.gin_i, ...), custom_call_target="tpu_custom_call" | custom-call | tf_op jit(solution)/shard_map/pallas_call | solution.py:534

commit v5 on v4

--- a/solution.py
+++ b/solution.py
@@ -21,6 +21,7 @@
 BLK = 64
 NZ, NSEQ, NQ = 16, 32, 16
 VM_BYTES = 40 * 2**20
+GROUP = 1
 CH = 4
 FACTOR = 1.0 / math.sqrt(NZ * NSEQ * ROWS)
 GELU_C = math.sqrt(2.0 / math.pi)
@@ -51,7 +52,7 @@
     lengths_hbm, placed_hbm, x_hbm, dy_hbm, w_hbm, gain_hbm, up_hbm, down_hbm,
     out_ref, gin_ref, gk_ref, gg_ref, fin,
     lengths, placed, x_ref, dy_ref, w_ref, gain_ref, up_v, down_v,
-    gath0, gath1, send_b, recv0, recv1, head, ext, gext, dep, rem_, normed_s, istd_s, scaled_s,
+    gath00, gath01, gath10, gath11, send_b, recv00, recv01, recv10, recv11, head, ext, gext, dep, rem_, normed_s, istd_s, scaled_s,
     gn_s, oacc_s, own, other, outbound, sib, tsum, r1, zs, r2, a1, kp, gp, kb, rk, rz, kf,
     ld_sem, a_s, a_r, b_s, b_r, c_s, c_r, p_s, p_r, z_s, z_r, y_s, y_r, q_s, q_r, f_s, f_r,
     k_s, k_r, kz_s, kz_r, kf_s, kf_r,
@@ -62,11 +63,33 @@
     q = lax.div(s, 2)
     yy = lax.rem(q, 4)
     xx = lax.div(q, 4)
-    g = xx * 2 + core
+    across = (xx * 2 + core, yy * 2 + core)
+    along = (yy, xx)
     gz = lax.div(z, 4)
     sibling = (z, q * 2 + 1 - core)
-    gath, recv = (gath0, gath1), (recv0, recv1)
-
+    gath = ((gath00, gath01), (gath10, gath11))
+    recv = ((recv00, recv01), (recv10, recv11))
+
+    x_to = [lax.rem(xx + i, 4) for i in range(4)]
+    y_to = [lax.rem(yy + i, 4) for i in range(4)]
+
+    def chip(k):
+        return x_to[k // 4] * 4 + y_to[k % 4]
+
+    def chip_back(k):
+        return x_to[-(k // 4) % 4] * 4 + y_to[-(k % 4) % 4]
+
+    bar = pltpu.get_barrier_semaphore()
+
+    def greet(zp, sp):
+        pl.semaphore_signal(bar, inc=1, device_id=(zp, sp), device_id_type=MESH)
+
+    for i in FAR_Z:
+        greet(lax.rem(z + i, NZ), s)
+    for k in FAR_Q:
+        greet(z, chip(k) * 2 + core)
+        greet(z, chip(k) * 2 + 1 - core)
+    greet(z, sibling[1])
     loads = [
         pltpu.make_async_copy(src, dst, ld_sem.at[i])
         for i, (src, dst) in enumerate((
@@ -76,35 +99,83 @@
     for copy in loads:
         copy.start()
 
-    bar = pltpu.get_barrier_semaphore()
-    for i in FAR_Z:
-        pl.semaphore_signal(bar, inc=1, device_id=(lax.rem(z + i, NZ), s), device_id_type=MESH)
-    loop(0, NSEQ - 1, lambda i: pl.semaphore_signal(
-        bar, inc=1, device_id=(z, lax.rem(s + 1 + lax.rem(i + 19, NSEQ - 1), NSEQ)), device_id_type=MESH))
+    pl.semaphore_wait(bar, NSEQ - 1 + NZ - 1)
+
+    def half(hf):
+        return pl.ds(hf * 128, 128)
+
+    def send_a(d, hf, i, src):
+        sp = ((xx * 4 + y_to[i]) if hf == 0 else (x_to[i] * 4 + yy)) * 2 + core
+        return remote(src.at[:, half(hf)], gath[d][hf].at[along[hf]], a_s.at[2 * d + hf, i], a_r.at[2 * d + hf, i],
+                      (z, sp))
+
+    def phase_a(d, src):
+        for i in (2, 1, 3):
+            for hf in range(2):
+                send_a(d, hf, i, src).start()
+
+    def phase_a_wait(d):
+        for i in range(1, 4):
+            for hf in range(2):
+                slot = gath[d][hf].at[lax.rem(along[hf] + 4 - i, 4)]
+                remote(slot, slot, a_s.at[2 * d + hf, i], a_r.at[2 * d + hf, i], sibling).wait_recv()
+
+    tail = x_hbm.at[pl.ds(ROWS - HALO, HALO), :]
+    phase_a(0, tail)
     loads[0].wait()
     loads[1].wait()
 
-    def target(i):
-        gt = lax.rem(g + i, 8)
-        return (lax.div(gt, 2) * 4 + yy) * 2 + lax.rem(gt, 2)
-
-    targets = [target(i) for i in range(8)]
-    at = [placed[0, t] for t in targets]
+    def target(hf, i):
+        gt = lax.rem(across[hf] + i, 8)
+        chip_of = lax.div(gt, 2) * 4 + yy if hf == 0 else xx * 4 + lax.div(gt, 2)
+        return chip_of * 2 + lax.rem(gt, 2)
+
+    targets = [[target(hf, i) for i in range(8)] for hf in range(2)]
+    at = [placed[0, t] for t in targets[0] + targets[1][1:]]
 
     def look(k, found):
         p = placed[0, k]
         return tuple(
-            jnp.where(p == at[i % 8] + (-1 if i < 8 else 1), k, f) for i, f in enumerate(found)
+            jnp.where(p == at[i % 15] + (-1 if i < 15 else 1), k, f) for i, f in enumerate(found)
         )
 
-    found = lax.fori_loop(0, NSEQ, look, (jnp.int32(0),) * 16)
-    before, after = found[:8], found[8:]
+    found = lax.fori_loop(0, NSEQ, look, (jnp.int32(0),) * 30)
+
+    def split(f):
+        return f[:8], f[:1] + f[8:]
+
+    before, after = split(found[:15]), split(found[15:])
+
+    def x_of(slot):
+        return lax.div(slot, 8)
 
     def y_of(slot):
         return lax.rem(lax.div(slot, 2), 4)
 
-    def g_of(slot):
-        return lax.div(slot, 8) * 2 + lax.rem(slot, 2)
+    def along_of(hf, slot):
+        return y_of(slot) if hf == 0 else x_of(slot)
+
+    def across_of(hf, slot):
+        return (x_of(slot) if hf == 0 else y_of(slot)) * 2 + lax.rem(slot, 2)
+
+    def send_b_(d, hf, i):
+        n = 2 * d + hf
+        return remote(send_b.at[n, i], recv[d][hf].at[across[hf]], b_s.at[n, i], b_r.at[n, i], (z, targets[hf][i]))
+
+    def phase_b(d, source):
+        for i in (4, 5, 3, 2, 6, 7, 1):
+            for hf in range(2):
+                send_b[2 * d + hf, i] = gath[d][hf][along_of(hf, source[hf][i])]
+                send_b_(d, hf, i).start()
+        for hf in range(2):
+            recv[d][hf][across[hf]] = gath[d][hf][along_of(hf, source[hf][0])]
+
+    def phase_b_wait(d, source):
+        for i in range(1, 8):
+            for hf in range(2):
+                slot = recv[d][hf].at[lax.rem(across[hf] + 8 - i, 8)]
+                remote(slot, slot, b_s.at[2 * d + hf, i], b_r.at[2 * d + hf, i], sibling).wait_recv()
+        return [recv[d][hf][across_of(hf, source[hf][0])].astype(F32) for hf in range(2)]
 
     pos = at[0] * ROWS + lax.broadcasted_iota(jnp.int32, (ROWS, 128), 0)
     ends, end = [], jnp.int32(0)
@@ -122,35 +193,10 @@
     loads[2].wait()
     for hf in range(2):
         ext[hf, HALO:, :] = x_ref[:, hf * 128:(hf + 1) * 128].astype(F32)
+    for hf in range(2):
+        gath[0][hf][along[hf]] = x_ref[ROWS - HALO:, hf * 128:(hf + 1) * 128]
     loads[3].wait()
     loads[4].wait()
-
-    def phase_a(d, src):
-        for i in range(1, 4):
-            peer = (xx * 4 + lax.rem(yy + i, 4)) * 2 + core
-            remote(src, gath[d].at[yy], a_s.at[d, i], a_r.at[d, i], (z, peer)).start()
-        gath[d][yy] = src[...]
-
-    def phase_a_wait(d):
-        for i in range(1, 4):
-            slot = gath[d].at[lax.rem(yy + 4 - i, 4)]
-            remote(slot, slot, a_s.at[d, i], a_r.at[d, i], sibling).wait_recv()
-
-    def phase_b(d, source):
-        for i in (4, 5, 3, 2, 6, 7, 1):
-            send_b[d, i] = gath[d][y_of(source[i])]
-            remote(send_b.at[d, i], recv[d].at[g], b_s.at[d, i], b_r.at[d, i], (z, targets[i])).start()
-        recv[d][g] = gath[d][y_of(source[0])]
-
-    def phase_b_wait(d, source):
-        for i in range(1, 8):
-            slot = recv[d].at[lax.rem(g + 8 - i, 8)]
-            remote(slot, slot, b_s.at[d, i], b_r.at[d, i], sibling).wait_recv()
-        return recv[d][g_of(source[0])].astype(F32)
-
-    pl.semaphore_wait(bar, NSEQ - 1 + NZ - 1)
-    tail = x_ref.at[pl.ds(ROWS - HALO, HALO), :]
-    phase_a(0, tail)
 
     def depthwise(src, base, sign, mask_ref, r0):
         m = mask_ref[r0:r0 + BLK, :]
@@ -178,15 +224,6 @@
 
     def rows16(i):
         return pl.ds(pl.multiple_of(i * 16, 16), 16)
-
-    x_to = [lax.rem(xx + i, 4) for i in range(4)]
-    y_to = [lax.rem(yy + i, 4) for i in range(4)]
-
-    def chip(k):
-        return x_to[k // 4] * 4 + y_to[k % 4]
-
-    def chip_back(k):
-        return x_to[-(k // 4) % 4] * 4 + y_to[-(k % 4) % 4]
 
     order = [lax.rem(gz + i, CH) for i in (2, 1, 3, 0)]
 
@@ -227,15 +264,15 @@
 
     def send_p(u, k):
         qp = chip(k)
-        return remote(tsum.at[pl.ds(2 * u, 2), rows16(qp), :], r1.at[u, k], p_s.at[u, k], p_r.at[u],
+        return remote(tsum.at[pl.ds(GROUP * u, GROUP), rows16(qp), :], r1.at[u, k], p_s.at[u, k], p_r.at[u],
                       (z, qp * 2 + core))
 
     def pair_stage(o):
         remote(sib.at[o], sib.at[o], c_s.at[o], c_r.at[o], sibling).wait_recv()
         tsum[o] = (own[o] + sib[o].astype(F32)).astype(BF16)
-        if o % 2:
+        if o % GROUP == GROUP - 1:
             for k in FAR_Q:
-                send_p(o // 2, k).start()
+                send_p(o // GROUP, k).start()
 
     def norm_back(r0):
         gn = gn_s[r0:r0 + BLK, :]
@@ -279,29 +316,30 @@
         forward_block(r0)
     for copy in loads[5:]:
         copy.wait()
-    feed_forward(0, BLK, ROWS)
     phase_a_wait(0)
     phase_b(0, before)
-    for o in range(1, CH):
+    for o in range(CH):
         feed_forward(o, BLK, ROWS)
-    for r0 in later:
-        norm_back(r0)
-    for r0 in later:
-        tap_block(r0)
 
     halo = phase_b_wait(0, before)
     for hf in range(2):
-        ext[hf, :HALO, :] = halo[:, hf * 128:(hf + 1) * 128]
+        ext[hf, :HALO, :] = halo[hf]
     forward_block(0)
     for o in range(CH):
         feed_forward(o, 0, BLK)
         if o:
             pair_stage(o - 1)
     pair_stage(CH - 1)
+    for r0 in later:
+        norm_back(r0)
     norm_back(0)
     for hf in range(2):
-        head[:, hf * 128:(hf + 1) * 128] = gext[hf, :HALO, :].astype(BF16)
+        rows = gext[hf, :HALO, :].astype(BF16)
+        head[:, hf * 128:(hf + 1) * 128] = rows
+        gath[1][hf][along[hf]] = rows
     phase_a(1, head)
+    for r0 in later:
+        tap_block(r0)
     tap_block(0)
     for hf in range(2):
         taps = jnp.sum(kp[hf], axis=1)
@@ -319,11 +357,11 @@
         i = lax.rem(zp - z + NZ, NZ)
         return remote(zs.at[zp], r2.at[i], z_s.at[i], z_r.at[0], (zp, s))
 
-    for u in range(CH // 2):
+    for u in range(CH // GROUP):
         got = r1.at[u, pl.ds(1, NQ - 1)]
         remote(got, got, p_s.at[u, 0], p_r.at[u], sibling).wait_recv()
-        for v in range(2):
-            o = 2 * u + v
+        for v in range(GROUP):
+            o = GROUP * u + v
             acc = tsum[o, rows16(q), :].astype(F32)
             for k in range(1, NQ):
                 acc = acc + r1[u, k, v].astype(F32)
@@ -400,7 +438,7 @@
 
     halo_g = phase_b_wait(1, after)
     for hf in range(2):
-        gext[hf, ROWS:, :] = halo_g[:, hf * 128:(hf + 1) * 128]
+        gext[hf, ROWS:, :] = halo_g[hf]
     back_block(3 * BLK)
 
     @pl.when(core == 0)
@@ -418,18 +456,19 @@
             kf.at[q], kf.at[q], kf_s.at[i], kf_r.at[q], (z, lax.rem(s + i, NSEQ))).start())
 
     def send_f(o):
-        half = fin.at[core, chunk_of(o)]
-        return remote(half, half, f_s.at[o], f_r.at[o], sibling)
+        part = fin.at[core, chunk_of(o)]
+        return remote(part, part, f_s.at[o], f_r.at[o], sibling)
 
     for d, src in ((0, tail), (1, head)):
-        for i in range(1, 4):
-            remote(src, src, a_s.at[d, i], a_r.at[d, i], sibling).wait_send()
-        for i in range(1, 8):
-            remote(send_b.at[d, i], send_b.at[d, i], b_s.at[d, i], b_r.at[d, i], sibling).wait_send()
+        for hf in range(2):
+            for i in range(1, 4):
+                send_a(d, hf, i, src).wait_send()
+            for i in range(1, 8):
+                send_b_(d, hf, i).wait_send()
     for o in range(CH):
         remote(outbound.at[o], outbound.at[o], c_s.at[o], c_r.at[o], sibling).wait_send()
     for k in range(1, NQ):
-        for u in range(CH // 2):
+        for u in range(CH // GROUP):
             send_p(u, k).wait_send()
         send_k(k).wait_send()
     for i in range(1, NZ):
@@ -458,8 +497,8 @@
         gk_ref[:, cols] = taps[:K, :].astype(BF16)
         gg_ref[:, cols] = taps[K:K + 1, :]
     for o in range(CH):
-        half = fin.at[1 - core, chunk_of(o)]
-        remote(half, half, f_s.at[o], f_r.at[o], sibling).wait_recv()
+        part = fin.at[1 - core, chunk_of(o)]
+        remote(part, part, f_s.at[o], f_r.at[o], sibling).wait_recv()
 
     for o in range(CH):
         for k in range(1, NQ):
@@ -506,8 +545,8 @@
             pltpu.SMEM((1, TRACES), jnp.int32), pltpu.SMEM((1, NSEQ), jnp.int32),
             V((ROWS, C), BF16), V((ROWS, C), BF16), V((K, C), F32), V((1, C), F32),
             V((C, HID), BF16), V((HID, C), BF16),
-            V((4, HALO, C), BF16), V((4, HALO, C), BF16), V((2, 8, HALO, C), BF16),
-            V((8, HALO, C), BF16), V((8, HALO, C), BF16),
+            *[V((4, HALO, 128), BF16)] * 4, V((4, 8, HALO, 128), BF16),
+            *[V((8, HALO, 128), BF16)] * 4,
             V((HALO, C), BF16),
             V((2, HALO + ROWS, 128), F32), V((2, ROWS + HALO, 128), F32),
             V((ROWS, 128), jnp.int32), V((ROWS, 128), jnp.int32),
@@ -515,12 +554,12 @@
             V((ROWS, C), F32), V((ROWS, C), F32),
             V((CH, 256, 256), F32), V((CH, 256, 256), F32),
             V((CH, 256, 256), BF16), V((CH, 256, 256), BF16), V((CH, 256, 256), BF16),
-            V((CH // 2, NQ, 2, 16, 256), BF16),
+            V((CH // GROUP, NQ, GROUP, 16, 256), BF16),
             V((NZ, 8, 128), F32), V((NZ, 8, 128), F32), V((NZ, 8, 128), F32),
             V((2, K, 8, 128), F32), V((8, C), F32), V((NQ, 8, 128), F32), V((NSEQ, 8, 128), F32),
             V((NZ, 8, 128), F32), V((NQ, 8, 128), F32),
-            D((8,)), D((2, 4)), D((2, 4)), D((2, 8)), D((2, 8)), D((CH,)), D((CH,)),
-            D((CH // 2, NQ)), D((CH // 2,)), D((NZ,)), D((1,)), D((NZ,)), D((NZ,)), D((CH, NQ)), D((CH, NQ)),
+            D((8,)), D((4, 4)), D((4, 4)), D((4, 8)), D((4, 8)), D((CH,)), D((CH,)),
+            D((CH // GROUP, NQ)), D((CH // GROUP,)), D((NZ,)), D((1,)), D((NZ,)), D((NZ,)), D((CH, NQ)), D((CH, NQ)),
             D((CH,)), D((CH,)), D((NQ,)), D((1,)), D((NZ,)), D((NZ,)), D((NSEQ,)), D((NQ,)),
         ],
         compiler_params=pltpu.CompilerParams(

time: 63.4 us -> 62.3 us (0.983)
  Pallas kernels: 62.7 us -> 61.5 us
    pallas_call x1, Pallas kernels: 61 us -> 59.9 us  [per_device(): pl.pallas_call(kernel, out_shape=(V((ROWS, C), BF16), V((ROWS, C), BF16),...]
where the time goes in v5:
time: 62.3 us; the launch traced here: 62.2 us
  Pallas kernels  61.5 us (99%)
  between operations  0.64 us (1%)
    pallas_call x1, Pallas kernels, per_device(): pl.pallas_call(kernel, out_shape=(V((ROWS, C), BF16), V((ROWS, C), BF16),...  59.9 us
    pallas_call x1, Pallas kernels, per_device(): pl.pallas_call(finish, out_shape=(jax.ShapeDtypeStruct((ROWS, C), BF16),...  1.66 us

profile of v5, /device:TPU:1, one launch (start us, length us, event | category | flops | bytes accessed | tf_op | source)
XLA Modules:
  0.0 62.2 jit_solution(5208827612724667463)
XLA Ops:
  0.6 59.9 %shard_map.127 = (bf16[256,256]{1,0:T(8,128)(2,1)S(1)}, bf16[256,256]{1,0:T(8,128)(2,1)S(1)}, bf16[51,256]{1,0:T(8,128)(2,1)S(1)}, f32[1,256]{1,0:T(1,128)S(1)}, bf16[2,4,256,256]{3,2,1,0:T(8,128)(2,1)S(1)}) custom-call(s32[1,8]{1,0:T(1,128)} %lengths_hbm.1, s32[1,32]{1,0:T(1,128)} %placed_hbm.1, bf16[256,256]{1,0:T(8,128)(2,1)} %bitcast.5, ...), custom_call_target="tpu_custom_call" | custom-call | tf_op jit(solution)/shard_map/pallas_call | solution.py:537
  60.5 1.7 %shard_map.128 = (bf16[256,256]{1,0:T(8,128)(2,1)}, bf16[256,256]{1,0:T(8,128)(2,1)}, bf16[51,256]{1,0:T(8,128)(2,1)}, bf16[256,1024]{1,0:T(8,128)(2,1)}, bf16[1...) custom-call(bf16[256,256]{1,0:T(8,128)(2,1)S(1)} %get-tuple-element.17.out_i, bf16[256,256]{1,0:T(8,128)(2,1)S(1)} %get-tuple-element.18.gin_i, ...), custom_call_target="tpu_custom_call" | custom-call | tf_op jit(solution)/shard_map/pallas_call | solution.py:573

commit v6 on v5

--- a/solution.py
+++ b/solution.py
@@ -329,10 +329,10 @@
         feed_forward(o, 0, BLK)
         if o:
             pair_stage(o - 1)
-    pair_stage(CH - 1)
     for r0 in later:
         norm_back(r0)
     norm_back(0)
+    pair_stage(CH - 1)
     for hf in range(2):
         rows = gext[hf, :HALO, :].astype(BF16)
         head[:, hf * 128:(hf + 1) * 128] = rows
@@ -496,9 +496,6 @@
         taps = jnp.concatenate([kf[2 * r + hf] for r in range(8)], axis=0)
         gk_ref[:, cols] = taps[:K, :].astype(BF16)
         gg_ref[:, cols] = taps[K:K + 1, :]
-    for o in range(CH):
-        part = fin.at[1 - core, chunk_of(o)]
-        remote(part, part, f_s.at[o], f_r.at[o], sibling).wait_recv()
 
     for o in range(CH):
         for k in range(1, NQ):
@@ -515,6 +512,10 @@
             rz.at[z], rz.at[z], kz_s.at[i], kz_r.at[i], sibling).wait_send())
         loop(1, NSEQ, lambda i: remote(
             kf.at[q], kf.at[q], kf_s.at[i], kf_r.at[q], sibling).wait_send())
+
+    for o in range(CH):
+        part = fin.at[1 - core, chunk_of(o)]
+        remote(part, part, f_s.at[o], f_r.at[o], sibling).wait_recv()
 
 
 def finish(out_i, gin_i, gk_i, gg_i, fin, out_o, gin_o, gk_o, gu_o, gd_o, gg_o, sem):

time: 62.3 us -> 62.2 us (level)
  no operation moved by 1% of the time
where the time goes in v6:
time: 62.2 us; the launch traced here: 62.1 us
  Pallas kernels  61.4 us (99%)
  between operations  0.64 us (1%)
    pallas_call x1, Pallas kernels, per_device(): pl.pallas_call(kernel, out_shape=(V((ROWS, C), BF16), V((ROWS, C), BF16),...  59.8 us
    pallas_call x1, Pallas kernels, per_device(): pl.pallas_call(finish, out_shape=(jax.ShapeDtypeStruct((ROWS, C), BF16),...  1.66 us

profile of v6, /device:TPU:1, one launch (start us, length us, event | category | flops | bytes accessed | tf_op | source)
XLA Modules:
  0.0 62.1 jit_solution(246479713315156862)
XLA Ops:
  0.6 59.8 %shard_map.127 = (bf16[256,256]{1,0:T(8,128)(2,1)S(1)}, bf16[256,256]{1,0:T(8,128)(2,1)S(1)}, bf16[51,256]{1,0:T(8,128)(2,1)S(1)}, f32[1,256]{1,0:T(1,128)S(1)}, bf16[2,4,256,256]{3,2,1,0:T(8,128)(2,1)S(1)}) custom-call(s32[1,8]{1,0:T(1,128)} %lengths_hbm.1, s32[1,32]{1,0:T(1,128)} %placed_hbm.1, bf16[256,256]{1,0:T(8,128)(2,1)} %bitcast.5, ...), custom_call_target="tpu_custom_call" | custom-call | tf_op jit(solution)/shard_map/pallas_call | solution.py:538
  60.4 1.7 %shard_map.128 = (bf16[256,256]{1,0:T(8,128)(2,1)}, bf16[256,256]{1,0:T(8,128)(2,1)}, bf16[51,256]{1,0:T(8,128)(2,1)}, bf16[256,1024]{1,0:T(8,128)(2,1)}, bf16[1...) custom-call(bf16[256,256]{1,0:T(8,128)(2,1)S(1)} %get-tuple-element.17.out_i, bf16[256,256]{1,0:T(8,128)(2,1)S(1)} %get-tuple-element.18.gin_i, ...), custom_call_target="tpu_custom_call" | custom-call | tf_op jit(solution)/shard_map/pallas_call | solution.py:574
